TPU v7x, 256 devices: a whole 4x4x8 slice. The times are simulated.
256 devices in a mesh: gx: 16 (over y, x), gy: 16 (over z, core).
Axes of the slice: x: 4, y: 4, z: 8, core: 2. Of those that a mesh axis runs over, the one named last changes fastest.
Arguments:
- innovation: float32 [68, 256, 4096], P(None, 'gx', 'gy'), may hold values from -6 to 6
- area: float32 [256, 4096], P('gx', 'gy'), may hold values from 0.5 to 2
- spread_sd: float32 [68, 64, 2048], P(None, 'gx', 'gy'), may hold values from 0.3 to 3
- smooth_coef: float32 [68], replicated, may hold values from 0.04 to 0.22
- obs_column: int32 [262144], P(('gx', 'gy')), may hold values from 0 to 511
- obs_weight: float32 [68, 262144], P(None, ('gx', 'gy')), may hold values from -0.75 to 0.75
- obs_precision: float32 [262144], P(('gx', 'gy')), may hold values from 0.5 to 4
- obs_live: int32 [262144], P(('gx', 'gy')), may hold values from 0 to 1, as said below
Outputs:
- fine_increment: float32 [68, 256, 4096], P(None, 'gx', 'gy')
- control: float32 [68, 64, 2048], P(None, 'gx', 'gy')
Inputs may be any that keep to these rules, and one draw needn't show every extreme that they name: obs_column is the index, inside the coarse tile of the tile that holds the slot, of the observed column, longitude-major (128 per row). `obs_live`: within each tile's block of 1024 slots the live ones come first; every block holds 128 or more, and some block is full.
All inputs are finite; a program needn't handle non-finite values.
Results may differ from a plain program's by a relative error of at most 0.0001.
Values sent between devices are 32-bit elements; how exact they have to be, the bound alone decides.
A program may use at most 64 MiB of HBM per device.

v0:
```python
import jax
import jax.numpy as jnp
from jax import lax
from jax.sharding import PartitionSpec as P

RX = 4
RY = 2
ITERS = 3


def extended_2(array, sides, width):
    for axis, dim in sides:
        count, length = (lax.axis_size(axis), array.shape[dim])
        up = [(i, (i + 1) % count) for i in range(count - 1)]
        down = [(j, i) for i, j in up]
        last = lax.slice_in_dim(array, length - width, length, axis=dim)
        leading = lax.slice_in_dim(array, 0, width, axis=dim)
        before = lax.ppermute(last, axis, up)
        after = lax.ppermute(leading, axis, down)
        array = jnp.concatenate([before, array, after], axis=dim)
    return array


def tap_weights(ratio):
    return [0.5 / (ratio + 1.0)] + [1.0 / (ratio + 1.0)] * ratio + [0.5 / (ratio + 1.0)]


def restrict(padded, coarse_x, coarse_y):
    weights_x = tap_weights(RX)
    weights_y = tap_weights(RY)
    along_x = weights_x[0] * padded[:, 0 : RX * (coarse_x - 1) + 1 : RX, :]
    for offset in range(1, RX + 2):
        along_x = (
            along_x
            + weights_x[offset] * padded[:, offset : offset + RX * (coarse_x - 1) + 1 : RX, :]
        )
    result = weights_y[0] * along_x[:, :, 0 : RY * (coarse_y - 1) + 1 : RY]
    for offset in range(1, RY + 2):
        result = (
            result
            + weights_y[offset] * along_x[:, :, offset : offset + RY * (coarse_y - 1) + 1 : RY]
        )
    return result


def spread(coarse):
    planes, coarse_x, coarse_y = coarse.shape
    weights_x = tap_weights(RX)
    weights_y = tap_weights(RY)
    middle = jnp.zeros((planes, coarse_x, RY * coarse_y + 2), jnp.float32)
    for offset in range(RY + 2):
        middle = middle.at[:, :, offset : offset + RY * (coarse_y - 1) + 1 : RY].add(
            weights_y[offset] * coarse
        )
    result = jnp.zeros((planes, RX * coarse_x + 2, RY * coarse_y + 2), jnp.float32)
    for offset in range(RX + 2):
        result = result.at[:, offset : offset + RX * (coarse_x - 1) + 1 : RX, :].add(
            weights_x[offset] * middle
        )
    return result


def smooth_padded(padded, smooth_coef):
    middle = padded[:, 1:-1, 1:-1]
    beside = padded[:, 2:, 1:-1] + padded[:, :-2, 1:-1] + padded[:, 1:-1, 2:] + padded[:, 1:-1, :-2]
    return (1.0 - 4.0 * smooth_coef)[:, None, None] * middle + smooth_coef[:, None, None] * beside


def observe(field, cells, obs_weight, obs_scale):
    columns = field.reshape(field.shape[0], -1)
    picked = jnp.take(columns, cells, axis=1)
    values = jnp.sum(obs_weight * picked, axis=0) * obs_scale
    return (
        jnp.zeros_like(columns).at[:, cells].add(obs_weight * values[None, :]).reshape(field.shape)
    )


def residual_norm(resid):
    return lax.psum(jnp.sum(resid * resid), ("gx", "gy"))


def per_device(
    innovation, area, spread_sd, smooth_coef, obs_column, obs_weight, obs_precision, obs_live
):
    planes, coarse_x, coarse_y = spread_sd.shape
    fine_x, fine_y = area.shape
    obs_scale = obs_precision * obs_live.astype(jnp.float32)

    def smooth_twice(field):
        for repeat in range(2):
            field = smooth_padded(extended_2(field, (("gx", 1), ("gy", 2)), 1), smooth_coef)
        return field

    weighted = innovation * area[None, :, :]
    padded_fine = extended_2(weighted, (("gx", 1), ("gy", 2)), 1)
    forcing = restrict(padded_fine, coarse_x, coarse_y)
    right_side = smooth_twice(spread_sd * forcing)
    control = jnp.zeros_like(right_side)
    resid = right_side
    direction = right_side
    norm_now = residual_norm(resid)
    for section in range(ITERS):
        pushed = spread_sd * smooth_twice(direction)
        hess_dir = direction + smooth_twice(
            spread_sd * observe(pushed, obs_column, obs_weight, obs_scale)
        )
        step_len = norm_now / lax.psum(jnp.sum(direction * hess_dir), ("gx", "gy"))
        control = control + step_len * direction
        resid = resid - step_len * hess_dir
        if section + 1 < ITERS:
            norm_next = residual_norm(resid)
            direction = resid + norm_next / norm_now * direction
            norm_now = norm_next
    increment = spread_sd * smooth_twice(control)
    extended = extended_2(increment, (("gx", 1), ("gy", 2)), 1)
    fine_ext = spread(extended)
    fine_increment = fine_ext[:, RX + 1 : RX + 1 + fine_x, RY + 1 : RY + 1 + fine_y]
    return (fine_increment, control)


def solution(mesh):
    return jax.shard_map(
        per_device,
        mesh=mesh,
        in_specs=(
            P(None, "gx", "gy"),
            P("gx", "gy"),
            P(None, "gx", "gy"),
            P(),
            P(("gx", "gy")),
            P(None, ("gx", "gy")),
            P(("gx", "gy")),
            P(("gx", "gy")),
        ),
        out_specs=(P(None, "gx", "gy"), P(None, "gx", "gy")),
        check_vma=False,
    )
```

profile of v0, /device:TPU:1, one launch (start us, length us, event | category | flops | bytes accessed | tf_op | source)
XLA Modules:
  0.0 843.7 jit_solution(12660146496590005178)
XLA Ops:
  2.6 3.9 collective-permute-start
  7.9 3.7 collective-permute-done.1
  12.3 5.5 collective-permute-start.2
  24.5 4.6 slice.518
  29.1 4.7 slice.517
  33.8 5.0 slice.516
  38.8 4.6 slice.515
  48.0 3.4 collective-permute-done.4
  53.4 3.6 collective-permute-start.7
  60.2 4.7 collective-permute-start.9
  66.2 3.4 collective-permute-done.8
  71.7 5.8 collective-permute-start.11
  80.6 3.8 collective-permute-start.13
  85.6 3.7 collective-permute-done.12
  91.5 5.5 collective-permute-start.15
  100.2 3.7 collective-permute-start.17
  105.3 3.6 collective-permute-done.16
  111.0 5.5 collective-permute-start.19
  123.2 6.1 scatter_custom_fusion
  129.5 3.8 collective-permute-start.21
  134.6 3.7 collective-permute-done.20
  140.3 5.5 collective-permute-start.23
  148.9 3.7 collective-permute-start.25
  154.0 3.7 collective-permute-done.24
  159.7 5.5 collective-permute-start.27
  169.1 89.3 %all-reduce = (f32[]{:T(128)}, f32[]{:T(128)}) all-reduce(f32[]{:T(128)} %get-tuple-element.12, f32[]{:T(128)} %get-tuple-element.11), channel_id=1, replica_groups=mesh['gx'=16,'gy'=16] {'gx','gy'}, use_global_device_ids=true, to_apply=%region_1.0 | all-reduce | flops 2 | bytes 16 | tf_op jit(solution)/shard_map/psum | solution.py:79
  260.5 73.9 %psum.44 = f32[]{:T(128)} all-reduce(f32[]{:T(128)} %get-tuple-element.17), channel_id=1, replica_groups=mesh['gx'=16,'gy'=16] {'gx','gy'}, use_global_device_ids=true, to_apply=%region_7.9 | all-reduce | flops 1 | bytes 8 | tf_op jit(solution)/shard_map/psum | solution.py:79
  339.7 3.4 collective-permute-done.28
  343.2 4.0 collective-permute-start.30
  356.5 3.7 collective-permute-done.32
  362.3 5.5 collective-permute-start.35
  374.5 6.1 scatter_custom_fusion.1
  380.7 5.2 collective-permute-start.37
  387.2 3.7 collective-permute-done.36
  393.0 5.5 collective-permute-start.39
  401.6 3.7 collective-permute-start.41
  406.7 3.7 collective-permute-done.40
  412.4 5.5 collective-permute-start.43
  421.6 80.7 %psum.45 = f32[]{:T(128)} all-reduce(f32[]{:T(128)} %get-tuple-element.15), channel_id=1, replica_groups=mesh['gx'=16,'gy'=16] {'gx','gy'}, use_global_device_ids=true, to_apply=%region_11.13 | all-reduce | flops 1 | bytes 8 | tf_op jit(solution)/shard_map/psum | solution.py:107
  504.4 74.3 %psum.46 = f32[]{:T(128)} all-reduce(f32[]{:T(128)} %multiply_reduce_fusion), channel_id=1, replica_groups=mesh['gx'=16,'gy'=16] {'gx','gy'}, use_global_device_ids=true, to_apply=%region_13.15 | all-reduce | flops 1 | bytes 8 | tf_op jit(solution)/shard_map/psum | solution.py:79
  583.8 3.4 collective-permute-done.44
  587.4 4.0 collective-permute-start.46
  600.6 3.7 collective-permute-done.48
  606.4 5.5 collective-permute-start.51
  618.6 6.1 scatter_custom_fusion.2
  624.8 5.2 collective-permute-start.53
  631.3 3.7 collective-permute-done.52
  637.1 5.5 collective-permute-start.55
  645.7 3.7 collective-permute-start.57
  651.0 3.5 collective-permute-done.56
  656.5 5.5 collective-permute-start.59
  665.7 80.7 %psum.47 = f32[]{:T(128)} all-reduce(f32[]{:T(128)} %fusion.3), channel_id=1, replica_groups=mesh['gx'=16,'gy'=16] {'gx','gy'}, use_global_device_ids=true, to_apply=%region_17.19 | all-reduce | flops 1 | bytes 8 | tf_op jit(solution)/shard_map/psum | solution.py:107
  751.9 3.4 collective-permute-done.60
  755.4 4.0 collective-permute-start.62
  769.3 3.4 collective-permute-done.64
  774.7 5.8 collective-permute-start.67
  783.6 3.9 collective-permute-start.68
  789.4 3.2 collective-permute-done.69
  792.7 5.5 collective-permute-start.70
  801.4 4.1 collective-permute-done.71
  806.6 5.5 scatter_fusion
  812.1 5.5 scatter_fusion.1
  817.6 5.5 scatter_fusion.2
  823.1 5.5 scatter_fusion.3
  (250 shorter events, 169.3 us)
Async XLA Ops:
  2.6 5.3 collective-permute-start
  6.5 5.1 collective-permute-start.1
  12.3 7.8 collective-permute-start.2
  18.2 5.0 collective-permute-start.3
  46.7 4.7 collective-permute-start.4
  51.5 7.3 collective-permute-start.6
  53.4 6.5 collective-permute-start.7
  60.2 6.0 collective-permute-start.9
  64.9 4.7 collective-permute-start.8
  69.7 9.4 %collective-permute-start.10 = (f32[68,6,1]{2,0,1:T(8,128)S(1)}, f32[68,6,1]{2,0,1:T(8,128)S(1)}, u32[]{:S(2)}, u32[]{:S(2)}) collective-permute-start(f32[68,6,1]{2,0,1:T(8,128)S(1)} %get-tuple-element.58), channel_id=1, source_target_pairs={{1,0},{2,1},{3,2},{4,3},{5,4},{6,5},{7,6},{8,7},{9,8},{10,9},{11,1... | collective-permute-start | bytes 4904 | tf_op jit(solution)/shard_map/ppermute | solution.py:19
  71.7 8.7 %collective-permute-start.11 = (f32[68,6,1]{2,0,1:T(8,128)S(1)}, f32[68,6,1]{2,0,1:T(8,128)S(1)}, u32[]{:S(2)}, u32[]{:S(2)}) collective-permute-start(f32[68,6,1]{2,0,1:T(8,128)S(1)} %get-tuple-element.59), channel_id=1, source_target_pairs={{0,1},{1,2},{2,3},{3,4},{4,5},{5,6},{6,7},{7,8},{8,9},{9,10},{10,1... | collective-permute-start | bytes 4904 | tf_op jit(solution)/shard_map/ppermute | solution.py:18
  80.6 5.1 collective-permute-start.13
  84.3 5.0 collective-permute-start.12
  89.5 9.3 %collective-permute-start.14 = (f32[68,6,1]{2,0,1:T(8,128)S(1)}, f32[68,6,1]{2,0,1:T(8,128)S(1)}, u32[]{:S(2)}, u32[]{:S(2)}) collective-permute-start(f32[68,6,1]{2,0,1:T(8,128)S(1)} %get-tuple-element.56), channel_id=1, source_target_pairs={{1,0},{2,1},{3,2},{4,3},{5,4},{6,5},{7,6},{8,7},{9,8},{10,9},{11,1... | collective-permute-start | bytes 4904 | tf_op jit(solution)/shard_map/ppermute | solution.py:19
  91.5 8.4 collective-permute-start.15
  100.2 5.1 collective-permute-start.17
  103.9 5.0 collective-permute-start.16
  109.0 9.1 %collective-permute-start.18 = (f32[68,6,1]{2,0,1:T(8,128)S(1)}, f32[68,6,1]{2,0,1:T(8,128)S(1)}, u32[]{:S(2)}, u32[]{:S(2)}) collective-permute-start(f32[68,6,1]{2,0,1:T(8,128)S(1)} %get-tuple-element.54), channel_id=1, source_target_pairs={{1,0},{2,1},{3,2},{4,3},{5,4},{6,5},{7,6},{8,7},{9,8},{10,9},{11,1... | collective-permute-start | bytes 4904 | tf_op jit(solution)/shard_map/ppermute | solution.py:19
  111.0 8.4 collective-permute-start.19
  129.5 5.1 collective-permute-start.21
  133.2 5.0 collective-permute-start.20
  138.4 9.2 %collective-permute-start.22 = (f32[68,6,1]{2,0,1:T(8,128)S(1)}, f32[68,6,1]{2,0,1:T(8,128)S(1)}, u32[]{:S(2)}, u32[]{:S(2)}) collective-permute-start(f32[68,6,1]{2,0,1:T(8,128)S(1)} %get-tuple-element.52), channel_id=1, source_target_pairs={{1,0},{2,1},{3,2},{4,3},{5,4},{6,5},{7,6},{8,7},{9,8},{10,9},{11,1... | collective-permute-start | bytes 4904 | tf_op jit(solution)/shard_map/ppermute | solution.py:19
  140.3 8.4 collective-permute-start.23
  148.9 5.1 collective-permute-start.25
  152.7 5.0 collective-permute-start.24
  157.8 9.1 %collective-permute-start.26 = (f32[68,6,1]{2,0,1:T(8,128)S(1)}, f32[68,6,1]{2,0,1:T(8,128)S(1)}, u32[]{:S(2)}, u32[]{:S(2)}) collective-permute-start(f32[68,6,1]{2,0,1:T(8,128)S(1)} %get-tuple-element.50), channel_id=1, source_target_pairs={{1,0},{2,1},{3,2},{4,3},{5,4},{6,5},{7,6},{8,7},{9,8},{10,9},{11,1... | collective-permute-start | bytes 4904 | tf_op jit(solution)/shard_map/ppermute | solution.py:19
  159.7 8.4 collective-permute-start.27
  338.4 4.7 collective-permute-start.28
  343.2 8.3 collective-permute-start.30
  347.2 5.5 collective-permute-start.31
  355.2 5.0 collective-permute-start.32
  360.3 9.1 %collective-permute-start.34 = (f32[68,6,1]{2,0,1:T(8,128)S(1)}, f32[68,6,1]{2,0,1:T(8,128)S(1)}, u32[]{:S(2)}, u32[]{:S(2)}) collective-permute-start(f32[68,6,1]{2,0,1:T(8,128)S(1)} %get-tuple-element.46), channel_id=1, source_target_pairs={{1,0},{2,1},{3,2},{4,3},{5,4},{6,5},{7,6},{8,7},{9,8},{10,9},{11,1... | collective-permute-start | bytes 4904 | tf_op jit(solution)/shard_map/ppermute | solution.py:19
  362.3 8.4 collective-permute-start.35
  380.7 6.5 collective-permute-start.37
  385.9 5.0 collective-permute-start.36
  391.1 9.2 %collective-permute-start.38 = (f32[68,6,1]{2,0,1:T(8,128)S(1)}, f32[68,6,1]{2,0,1:T(8,128)S(1)}, u32[]{:S(2)}, u32[]{:S(2)}) collective-permute-start(f32[68,6,1]{2,0,1:T(8,128)S(1)} %get-tuple-element.44), channel_id=1, source_target_pairs={{1,0},{2,1},{3,2},{4,3},{5,4},{6,5},{7,6},{8,7},{9,8},{10,9},{11,1... | collective-permute-start | bytes 4904 | tf_op jit(solution)/shard_map/ppermute | solution.py:19
  393.0 8.4 collective-permute-start.39
  401.6 5.1 collective-permute-start.41
  405.4 5.0 collective-permute-start.40
  410.5 9.1 %collective-permute-start.42 = (f32[68,6,1]{2,0,1:T(8,128)S(1)}, f32[68,6,1]{2,0,1:T(8,128)S(1)}, u32[]{:S(2)}, u32[]{:S(2)}) collective-permute-start(f32[68,6,1]{2,0,1:T(8,128)S(1)} %get-tuple-element.42), channel_id=1, source_target_pairs={{1,0},{2,1},{3,2},{4,3},{5,4},{6,5},{7,6},{8,7},{9,8},{10,9},{11,1... | collective-permute-start | bytes 4904 | tf_op jit(solution)/shard_map/ppermute | solution.py:19
  412.4 8.4 collective-permute-start.43
  587.4 8.3 collective-permute-start.46
  591.4 5.5 collective-permute-start.47
  599.3 5.0 collective-permute-start.48
  604.4 9.1 %collective-permute-start.50 = (f32[68,6,1]{2,0,1:T(8,128)S(1)}, f32[68,6,1]{2,0,1:T(8,128)S(1)}, u32[]{:S(2)}, u32[]{:S(2)}) collective-permute-start(f32[68,6,1]{2,0,1:T(8,128)S(1)} %get-tuple-element.38), channel_id=1, source_target_pairs={{1,0},{2,1},{3,2},{4,3},{5,4},{6,5},{7,6},{8,7},{9,8},{10,9},{11,1... | collective-permute-start | bytes 4904 | tf_op jit(solution)/shard_map/ppermute | solution.py:19
  606.4 8.4 collective-permute-start.51
  624.8 6.5 collective-permute-start.53
  630.0 5.0 collective-permute-start.52
  635.2 9.2 %collective-permute-start.54 = (f32[68,6,1]{2,0,1:T(8,128)S(1)}, f32[68,6,1]{2,0,1:T(8,128)S(1)}, u32[]{:S(2)}, u32[]{:S(2)}) collective-permute-start(f32[68,6,1]{2,0,1:T(8,128)S(1)} %get-tuple-element.36), channel_id=1, source_target_pairs={{1,0},{2,1},{3,2},{4,3},{5,4},{6,5},{7,6},{8,7},{9,8},{10,9},{11,1... | collective-permute-start | bytes 4904 | tf_op jit(solution)/shard_map/ppermute | solution.py:19
  637.1 8.4 collective-permute-start.55
  645.7 5.3 collective-permute-start.57
  649.5 5.0 collective-permute-start.56
  654.6 9.1 %collective-permute-start.58 = (f32[68,6,1]{2,0,1:T(8,128)S(1)}, f32[68,6,1]{2,0,1:T(8,128)S(1)}, u32[]{:S(2)}, u32[]{:S(2)}) collective-permute-start(f32[68,6,1]{2,0,1:T(8,128)S(1)} %get-tuple-element.34), channel_id=1, source_target_pairs={{1,0},{2,1},{3,2},{4,3},{5,4},{6,5},{7,6},{8,7},{9,8},{10,9},{11,1... | collective-permute-start | bytes 4904 | tf_op jit(solution)/shard_map/ppermute | solution.py:19
  656.5 8.4 collective-permute-start.59
  750.6 4.7 collective-permute-start.60
  755.4 8.0 collective-permute-start.62
  759.4 5.2 collective-permute-start.63
  768.0 4.7 collective-permute-start.64
  772.8 9.4 %collective-permute-start.66 = (f32[68,6,1]{2,0,1:T(8,128)S(1)}, f32[68,6,1]{2,0,1:T(8,128)S(1)}, u32[]{:S(2)}, u32[]{:S(2)}) collective-permute-start(f32[68,6,1]{2,0,1:T(8,128)S(1)} %get-tuple-element.30), channel_id=1, source_target_pairs={{1,0},{2,1},{3,2},{4,3},{5,4},{6,5},{7,6},{8,7},{9,8},{10,9},{11,1... | collective-permute-start | bytes 4904 | tf_op jit(solution)/shard_map/ppermute | solution.py:19
  774.7 8.7 %collective-permute-start.67 = (f32[68,6,1]{2,0,1:T(8,128)S(1)}, f32[68,6,1]{2,0,1:T(8,128)S(1)}, u32[]{:S(2)}, u32[]{:S(2)}) collective-permute-start(f32[68,6,1]{2,0,1:T(8,128)S(1)} %get-tuple-element.31), channel_id=1, source_target_pairs={{0,1},{1,2},{2,3},{3,4},{4,5},{5,6},{6,7},{7,8},{8,9},{9,10},{10,1... | collective-permute-start | bytes 4904 | tf_op jit(solution)/shard_map/ppermute | solution.py:18
  783.6 5.7 collective-permute-start.68
  787.5 5.0 collective-permute-start.69
  792.7 8.7 %collective-permute-start.70 = (f32[68,6,1]{2,0,1:T(8,128)S(1)}, f32[68,6,1]{2,0,1:T(8,128)S(1)}, u32[]{:S(2)}, u32[]{:S(2)}) collective-permute-start(f32[68,6,1]{2,0,1:T(8,128)S(1)} %get-tuple-element.28), channel_id=1, source_target_pairs={{0,1},{1,2},{2,3},{3,4},{4,5},{5,6},{6,7},{7,8},{8,9},{9,10},{10,1... | collective-permute-start | bytes 4904 | tf_op jit(solution)/shard_map/ppermute | solution.py:18
  798.2 7.3 collective-permute-start.71
  (16 other events, 129.9 us)
where the time goes:
time: 860 us; the launch traced here: 844 us
  blocking collectives  399 us (46%)
  starting transfers between devices  217 us (25%)
  waiting for transfers between devices  116 us (13%)
  other arithmetic  63.1 us (7%)
  local copies, waits for them, and re-layouts  39.1 us (5%)
  between operations  9.39 us (1%)
    psum x3, blocking collectives, residual_norm(): return lax.psum(jnp.sum(resid * resid), ('gx', 'gy'))  238 us
    psum x2, blocking collectives, per_device(): step_len = norm_now / lax.psum(jnp.sum(direction * hess_dir), ('gx', 'gy'))  161 us
    ppermute x36, starting transfers between devices, extended_2(): before = lax.ppermute(last, axis, up)  153 us
    ppermute x36, waiting for transfers between devices, extended_2(): after = lax.ppermute(leading, axis, down)  97 us
    ppermute x36, starting transfers between devices, extended_2(): after = lax.ppermute(leading, axis, down)  64.4 us
    scatter-add x4, other arithmetic, spread(): middle.at[:, :, offset:offset + RY * (coarse_y - 1) + 1:RY]  22 us
    ppermute x36, waiting for transfers between devices, extended_2(): before = lax.ppermute(last, axis, up)  19 us
    scatter-add x3, other arithmetic, observe(): jnp.zeros_like(columns).at[:, cells].add(obs_weight * values[None, :])  18.3 us
  transfers between devices with their start and end apart: 72, of which 53 were waited for; matrix products, arithmetic and copies ran while one was open for 0% of the time, Pallas kernels for 0%

commit v1 on v0

v1 whole, which is shorter than its diff:
```python
import functools

import jax
import jax.numpy as jnp
from jax import lax
from jax.experimental import pallas as pl
from jax.experimental.pallas import tpu as pltpu
from jax.sharding import PartitionSpec as P

F32 = jnp.float32
BF16 = jnp.bfloat16
MESH = pl.DeviceIdType.MESH
PLANES = 68
PAD = 72
MPAD = 80
GROUPS = PAD // 8
SIDES = [(sx, sy) for sx in (-1, 0, 1) for sy in (-1, 1)]


def pieces(x):
    high = x.astype(BF16)
    rest = x - high.astype(F32)
    middle = rest.astype(BF16)
    low = (rest - middle.astype(F32)).astype(BF16)
    return jnp.concatenate([high, middle, low], axis=0)


def dot(a, b):
    return jnp.dot(a, b, preferred_element_type=F32)


def iota(shape, dim):
    return lax.broadcasted_iota(jnp.int32, shape, dim)


def tap(offset, ratio):
    inner = (offset >= 0) & (offset < ratio)
    ends = (offset == -1) | (offset == ratio)
    return jnp.where(inner, 2.0, jnp.where(ends, 1.0, 0.0))


def coarse_lane(lane):
    return jnp.where(lane == 255, -1, lane)


def roll(x, shift):
    return pltpu.roll(x, shift % 128, x.ndim - 1)


def beside(low, high, lane):
    low_up, low_down = roll(low, 1), roll(low, 127)
    high_up, high_down = roll(high, 1), roll(high, 127)
    first, last = lane == 0, lane == 127
    of_low = jnp.where(first, high_up, low_up) + jnp.where(last, high_down, low_down)
    of_high = jnp.where(first, low_up, high_up) + jnp.where(last, low_down, high_down)
    return of_low, of_high


def solve(
    nx,
    ny,
    inn_hbm,
    area_hbm,
    sd_hbm,
    coef_ref,
    col_ref,
    weight_hbm,
    prec_ref,
    live_ref,
    inc_low,
    inc_high,
    ctl,
    inn,
    area,
    sd_in,
    sd,
    weight,
    coef_a,
    coef_b,
    pick,
    place,
    taps_y,
    along,
    rest_low,
    rest_high,
    rim_in,
    field,
    packed,
    packed_in,
    res_low,
    res_high,
    dir_low,
    dir_high,
    ured,
    gathered,
    scaled,
    msg_a,
    msg_b,
    slots_a,
    slots_b,
    in_sems,
    x_send,
    x_recv,
    p_send,
    p_recv,
    a_send,
    a_recv,
    b_send,
    b_recv,
):
    gx, gy = lax.axis_index("gx"), lax.axis_index("gy")

    def at(dx, dy):
        return (lax.rem(gx + dx + nx, nx), lax.rem(gy + dy + ny, ny))

    loads = [
        pltpu.make_async_copy(inn_hbm, inn.at[pl.ds(0, PLANES)], in_sems.at[0]),
        pltpu.make_async_copy(area_hbm, area, in_sems.at[1]),
        pltpu.make_async_copy(sd_hbm, sd_in, in_sems.at[2]),
        pltpu.make_async_copy(weight_hbm, weight, in_sems.at[3]),
    ]
    for load in loads:
        load.start()

    barrier = pltpu.get_barrier_semaphore()
    partners = [at(0, o) for o in range(1, ny)] + [at(o, 0) for o in range(1, nx)]
    partners += [at(dx, dy) for dx in (-1, 1) for dy in (-1, 1)]
    for partner in partners:
        pl.semaphore_signal(barrier, inc=1, device_id=partner, device_id_type=MESH)

    lane8 = iota((8, 128), 1)
    left_ok, right_ok = gx > 0, gx < nx - 1
    low_ok, high_ok = gy > 0, gy < ny - 1
    edge_f = jnp.where(lane8 < 64, jnp.where(high_ok, 1.0, 0.0), jnp.where(low_ok, 1.0, 0.0))
    left_f, right_f = jnp.where(left_ok, 1.0, 0.0), jnp.where(right_ok, 1.0, 0.0)

    inn[PLANES:] = jnp.zeros((PAD - PLANES, 16, 256), F32)
    gathered[PAD:] = jnp.zeros((MPAD - PAD, 512), F32)
    diagonal = iota((PAD, PLANES), 0) == iota((PAD, PLANES), 1)
    coef = jnp.sum(
        jnp.where(diagonal, jnp.broadcast_to(coef_ref[...], (PAD, PLANES)), 0.0),
        axis=1,
        keepdims=True,
    )
    coef_b[...] = jnp.broadcast_to(coef, (PAD, 128))
    coef_a[...] = jnp.broadcast_to(1.0 - 4.0 * coef, (PAD, 128))

    out_row, in_row = iota((48, 384), 0), iota((48, 384), 1) & 127
    same = (out_row & 7) == (in_row >> 4)
    off = (in_row & 15) - 4 * ((out_row >> 3) - 1)
    taps_x = jnp.where(same, tap(off, 4), 0.0).astype(BF16)
    taps_y[...] = tap(iota((256, 256), 0) - 2 * coarse_lane(iota((256, 256), 1)), 2).astype(BF16)

    loads[0].wait()
    loads[1].wait()

    def restrict_x(g, carry):
        at_g = pl.ds(pl.multiple_of(g * 8, 8), 8)
        block = (inn[at_g] * area[...][None]).reshape(128, 256)
        along[:, at_g, :] = dot(taps_x, pieces(block)).reshape(6, 8, 256)
        return carry

    lax.fori_loop(0, GROUPS, restrict_x, 0, unroll=3)
    part = dot(pieces(along[...].reshape(6 * PAD, 256)), taps_y[...])
    part = (part[: 6 * PAD] + part[6 * PAD : 12 * PAD] + part[12 * PAD :]) * (1.0 / 60.0)
    rest_low[...] = part[:, :128].reshape(6, PAD, 128)
    rest_high[...] = part[:, 128:].reshape(6, PAD, 128)

    edge = jnp.zeros((PAD, 128), F32)
    for r in range(6):
        edge = edge + roll(rest_high[r], 1 + 2 * r)
    packed[0] = edge

    pl.semaphore_wait(barrier, len(partners))

    def remote(source, target, send, recv, device):
        copy = pltpu.make_async_remote_copy(
            src_ref=source,
            dst_ref=target,
            send_sem=send,
            recv_sem=recv,
            device_id=device,
            device_id_type=MESH,
        )
        copy.start()
        return copy

    sent = []

    def exchange(e, to_left, at_right, to_right, at_left):
        copies = [
            remote(to_left, at_right, x_send.at[e, 0], x_recv.at[e, 1], at(-1, 0)),
            remote(to_right, at_left, x_send.at[e, 1], x_recv.at[e, 0], at(1, 0)),
        ]
        for n, (sx, sy) in enumerate(SIDES):
            copies.append(
                remote(
                    packed.at[e], packed_in.at[e, n], p_send.at[e, n], p_recv.at[e, n], at(-sx, -sy)
                )
            )
        sent.extend(copies)
        return copies

    def arrived(copies):
        for copy in copies:
            copy.wait_recv()

    def sides(e, at_g, above):
        result = []
        for sx, ok in ((-1, left_ok), (0, None), (1, right_ok)):
            n = 2 * (sx + 1)
            both = jnp.where(above, packed_in[e, n + 1, at_g, :], packed_in[e, n, at_g, :])
            inside = jnp.where(above, jnp.where(high_ok, 1.0, 0.0), jnp.where(low_ok, 1.0, 0.0))
            if ok is not None:
                inside = inside * jnp.where(ok, 1.0, 0.0)
            result.append(jnp.where(inside > 0.5, both, 0.0))
        return result

    copies = exchange(0, rest_low.at[0], rim_in.at[1], rest_low.at[5], rim_in.at[0])

    loads[2].wait()
    loads[3].wait()
    for i in range(4):
        sd[i, :PLANES] = sd_in[:, i, :]
        sd[i, PLANES:] = jnp.zeros((PAD - PLANES, 128), F32)
    cols = col_ref[...]
    cols_t = jnp.transpose(jnp.concatenate([cols.astype(F32), jnp.zeros((120, 128), F32)], axis=0))
    column = iota((512, 128), 0)
    for a in range(8):
        k = pl.ds(128 * a, 128)
        pick[:, k] = jnp.where(column == cols[a : a + 1], 1.0, 0.0).astype(BF16)
        of_slot = jnp.broadcast_to(cols_t[:, a : a + 1], (128, 512))
        place[k, :] = jnp.where(of_slot == iota((128, 512), 1).astype(F32), 1.0, 0.0).astype(BF16)
    obs_scale = prec_ref[...] * live_ref[...].astype(F32)

    arrived(copies)

    def force(g, carry):
        at_g = pl.ds(pl.multiple_of(g * 8, 8), 8)
        rim = sides(0, at_g, (lane8 & 1) == 0)
        ends = (lane8 == 0) | (lane8 == 127)
        for i in range(4):
            value = rest_low[i + 1, at_g, :]
            tails = roll(rim[1], -(2 * (i + 1) + 1))
            if i == 0:
                value = value + rim_in[0, at_g, :] * left_f
                tails = tails + roll(rim[0], -11)
            if i == 3:
                value = value + rim_in[1, at_g, :] * right_f
                tails = tails + roll(rim[2], -1)
            value = value + jnp.where(ends, tails, 0.0)
            field[0, 4 + i, at_g, :] = sd[i, at_g, :] * value
        return carry

    lax.fori_loop(0, GROUPS, force, 0, unroll=3)

    def pack_and_send(e):
        def pack(g, carry):
            at_g = pl.ds(pl.multiple_of(g * 8, 8), 8)
            value = jnp.zeros((8, 128), F32)
            for i in range(4):
                value = jnp.where(
                    (lane8 >> 3) == i, roll(field[e, 4 + i, at_g, :], 4 + 8 * i), value
                )
            packed[1 + e, at_g, :] = value
            return carry

        lax.fori_loop(0, GROUPS, pack, 0, unroll=9)
        own = field.at[e, pl.ds(4, 4)]
        return exchange(1 + e, own, field.at[e, pl.ds(8, 4)], own, field.at[e, pl.ds(0, 4)])

    def smooth(rows, first, coefs):
        result = []
        for n in range(1, len(rows) - 1):
            i = first + n
            a, b, a_high, b_high = coefs[0 if i < 0 else 1 if i < 4 else 2]
            (low, high), before, after = rows[n], rows[n - 1], rows[n + 1]
            of_low, of_high = beside(low, high, lane8)
            of_low = of_low + before[0] + after[0]
            of_high = of_high + before[1] + after[1]
            result.append((a * low + b * of_low, a_high * high + b_high * of_high))
        return result

    def smooth_step(e, alpha, beta):
        def step(g, norm):
            at_g = pl.ds(pl.multiple_of(g * 8, 8), 8)
            odd = (lane8 & 4) == 4
            tails = sides(1 + e, at_g, odd)
            rows = []
            for r in range(12):
                low = field[e, r, at_g, :]
                if r < 4:
                    low = jnp.where(left_f > 0.5, low, 0.0)
                if r >= 8:
                    low = jnp.where(right_f > 0.5, low, 0.0)
                rows.append((low, roll(tails[r // 4], -(8 * (r % 4) + 4))))
            a, b = coef_a[at_g, :], coef_b[at_g, :]
            coefs = [
                (a * f, b * f, a * f * edge_f, b * f * edge_f) for f in (left_f, F32(1.0), right_f)
            ]
            rows = smooth(smooth(rows, -4, coefs), -3, coefs)
            values = []
            for q, (low, high) in enumerate(rows):
                if e > 0:
                    old_low, old_high = res_low[e - 1, q, at_g, :], res_high[e - 1, q, at_g, :]
                    low, high = low + old_low, high + old_high
                    if e > 1:
                        low = low + beta * dir_low[q, at_g, :]
                        high = high + beta * dir_high[q, at_g, :]
                    else:
                        dir_low[q, at_g, :] = low
                        dir_high[q, at_g, :] = high
                    low, high = old_low - alpha * low, old_high - alpha * high
                res_low[e, q, at_g, :] = low
                res_high[e, q, at_g, :] = high
                values.append((low, high))
                if 2 <= q < 6:
                    norm = norm + low * low
            values = smooth(smooth(values, -2, coefs), -1, coefs)
            for i, (low, _) in enumerate(values):
                pushed = sd[i, at_g, :] * low
                ured[1 + i, e, at_g, :] = pushed
                gathered[at_g, pl.ds(128 * i, 128)] = pushed
            return norm

        return lax.fori_loop(0, GROUPS, step, jnp.zeros((8, 128), F32), unroll=1)

    def observe(e, norm):
        left = pieces(gathered[...])
        total = jnp.zeros((1, 128), F32)
        live = iota((PLANES, 256), 0) >= 0
        for n in range(4):
            k = pl.ds(256 * n, 256)
            taken = dot(left, pick[:, k])
            taken = taken[:MPAD] + taken[MPAD : 2 * MPAD] + taken[2 * MPAD :]
            w = weight[:, k]
            seen = jnp.sum(w * taken[:PLANES], axis=0, keepdims=True)
            scale = jnp.concatenate(
                [obs_scale[2 * n : 2 * n + 1], obs_scale[2 * n + 1 : 2 * n + 2]], axis=1
            )
            value = scale * seen
            square = value * seen
            total = total + square[:, :128] + square[:, 128:]
            if e < 2:
                back = jnp.concatenate([w * value, jnp.zeros((MPAD - PLANES, 256), F32)], axis=0)
                scaled[:, k] = pieces(back)
        msg_a[e] = jnp.concatenate([jnp.sum(norm, axis=0, keepdims=True), total], axis=0)

    def put_back(e):
        for h in range(2):
            value = dot(scaled[...], place[:, 256 * h : 256 * h + 256])
            value = value[:PAD] + value[MPAD : MPAD + PAD] + value[2 * MPAD : 2 * MPAD + PAD]
            for i in (2 * h, 2 * h + 1):
                field[e, 4 + i] = sd[i] * value[:, 128 * (i % 2) : 128 * (i % 2) + 128]

    def reduce_start(k, msg, slots, send, recv, count, mine, partner):
        slots[k, mine] = msg[k]
        for o in range(1, count):
            remote(msg.at[k], slots.at[k, mine], send.at[k], recv.at[k], partner(o))

    def reduce_end(k, slots, send, recv, count, partner):
        several = slots.at[k, pl.ds(0, count - 1)]
        whole = pltpu.make_async_remote_copy(
            src_ref=several,
            dst_ref=several,
            send_sem=send.at[k],
            recv_sem=recv.at[k],
            device_id=partner(1),
            device_id_type=MESH,
        )
        whole.wait_recv()
        whole.wait_send()
        total = slots[k, 0]
        for o in range(1, count):
            total = total + slots[k, o]
        return total

    def start_a(k):
        reduce_start(k, msg_a, slots_a, a_send, a_recv, ny, gy, lambda o: at(0, o))

    def turn(k):
        msg_b[k] = reduce_end(k, slots_a, a_send, a_recv, ny, lambda o: at(0, o))
        reduce_start(k, msg_b, slots_b, b_send, b_recv, nx, gx, lambda o: at(o, 0))

    def end_b(k):
        total = reduce_end(k, slots_b, b_send, b_recv, nx, lambda o: at(o, 0))
        total = jnp.sum(total, axis=1, keepdims=True)
        gamma = jnp.broadcast_to(total[0:1], (8, 128))
        return gamma, gamma + jnp.broadcast_to(total[1:2], (8, 128))

    copies = pack_and_send(0)
    arrived(copies)
    norm = smooth_step(0, None, None)
    observe(0, norm)
    start_a(0)
    put_back(1)
    copies = pack_and_send(1)
    turn(0)
    arrived(copies)
    gamma0, delta0 = end_b(0)
    alpha0 = gamma0 / delta0

    norm = smooth_step(1, alpha0, None)
    observe(1, norm)
    start_a(1)
    put_back(2)
    copies = pack_and_send(2)
    turn(1)
    arrived(copies)
    gamma1, delta1 = end_b(1)
    beta1 = gamma1 / gamma0
    alpha1 = gamma1 / (delta1 - beta1 * gamma1 / alpha0)

    norm = smooth_step(2, alpha1, beta1)
    observe(2, norm)
    start_a(2)

    def pack_rims(g, carry):
        at_g = pl.ds(pl.multiple_of(g * 8, 8), 8)
        value = jnp.zeros((8, 128), F32)
        for v in range(3):
            for i in range(4):
                n = 4 * v + i
                value = jnp.where((lane8 >> 1) == n, roll(ured[1 + i, v, at_g, :], 1 + 2 * n), value)
        packed[4, at_g, :] = value
        return carry

    lax.fori_loop(0, GROUPS, pack_rims, 0, unroll=3)
    copies = exchange(4, ured.at[1], ured.at[5], ured.at[4], ured.at[0])
    turn(2)
    arrived(copies)
    gamma2, delta2 = end_b(2)
    beta2 = gamma2 / gamma1
    alpha2 = gamma2 / (delta2 - beta2 * gamma2 / alpha1)
    parts = [alpha0 + beta1 * (alpha1 + alpha2 * beta2), alpha1 + alpha2 * beta2, alpha2]

    def combine(g, carry):
        at_g = pl.ds(pl.multiple_of(g * 8, 8), 8)
        for i in range(4):
            ctl[i, at_g, :] = (
                parts[0] * res_low[0, 2 + i, at_g, :]
                + parts[1] * res_low[1, 2 + i, at_g, :]
                + parts[2] * res_low[2, 2 + i, at_g, :]
            )
        for r in range(6):
            value = (
                parts[0] * ured[r, 0, at_g, :]
                + parts[1] * ured[r, 1, at_g, :]
                + parts[2] * ured[r, 2, at_g, :]
            )
            if r == 0:
                value = jnp.where(left_f > 0.5, value, 0.0)
            if r == 5:
                value = jnp.where(right_f > 0.5, value, 0.0)
            inc_low[r, at_g, :] = value
        odd = (lane8 & 1) == 1
        of_lane = jnp.where(lane8 < 8, parts[0], jnp.where(lane8 < 16, parts[1], parts[2]))
        tails = []
        for value in sides(4, at_g, odd):
            value = value * of_lane
            tails.append(value + roll(value, -8) + roll(value, -16))
        for r in range(6):
            i = (r - 1) % 4
            sx = 0 if r == 0 else 2 if r == 5 else 1
            inc_high[r, at_g, :] = roll(tails[sx], -(2 * i + 1))
        return carry

    lax.fori_loop(0, GROUPS, combine, 0, unroll=1)
    for copy in sent:
        copy.wait_send()


def finish(inc_low, inc_high, ctl, fine_hbm, control, along, fine, sems):
    lane, row = iota((256, 256), 0), iota((256, 256), 1)
    taps_y = tap(row - 2 * coarse_lane(lane), 2).astype(BF16)
    low, high = inc_low[...].reshape(6 * PAD, 128), inc_high[...].reshape(6 * PAD, 128)
    high = jnp.where((iota(high.shape, 1) == 0) | (iota(high.shape, 1) == 127), high, 0.0)
    wide = dot(pieces(jnp.concatenate([low, high], axis=1)), taps_y)
    wide = (wide[: 6 * PAD] + wide[6 * PAD : 12 * PAD] + wide[12 * PAD :]) * (1.0 / 60.0)
    along[...] = wide.reshape(6, PAD, 256)

    out_row, n = iota((128, 48), 0), iota((128, 48), 1)
    off = (out_row & 15) - 4 * ((n >> 3) - 1)
    taps_x = jnp.where((n & 7) == (out_row >> 4), tap(off, 4), 0.0).astype(BF16)
    taps_x = jnp.concatenate([taps_x] * 3, axis=1)
    copies = []
    for g in range(GROUPS):
        count = min(8, PLANES - 8 * g)
        block = dot(taps_x, pieces(along[:, 8 * g : 8 * g + 8, :].reshape(48, 256)))
        fine[8 * g : 8 * g + 8] = block.reshape(8, 16, 256)
        planes = pl.ds(8 * g, count)
        copies.append(pltpu.make_async_copy(fine.at[planes], fine_hbm.at[planes], sems.at[g]))
        copies[-1].start()
    for i in range(4):
        control[:, i, :] = ctl[i, :PLANES, :]
    for copy in copies:
        copy.wait()


def per_device(
    nx, ny, innovation, area, spread_sd, smooth_coef, obs_column, obs_weight, obs_precision, obs_live
):
    vmem, anywhere = pl.BlockSpec(memory_space=pltpu.VMEM), pl.BlockSpec(memory_space=pl.ANY)
    dma = pltpu.SemaphoreType.DMA
    inc_low, inc_high, ctl = pl.pallas_call(
        functools.partial(solve, nx, ny),
        out_shape=[
            jax.ShapeDtypeStruct((6, PAD, 128), F32),
            jax.ShapeDtypeStruct((6, PAD, 128), F32),
            jax.ShapeDtypeStruct((4, PAD, 128), F32),
        ],
        in_specs=[anywhere, anywhere, anywhere, vmem, vmem, anywhere, vmem, vmem],
        out_specs=[vmem, vmem, vmem],
        scratch_shapes=[
            pltpu.VMEM((PAD, 16, 256), F32),
            pltpu.VMEM((16, 256), F32),
            pltpu.VMEM((PLANES, 4, 128), F32),
            pltpu.VMEM((4, PAD, 128), F32),
            pltpu.VMEM((PLANES, 1024), F32),
            pltpu.VMEM((PAD, 128), F32),
            pltpu.VMEM((PAD, 128), F32),
            pltpu.VMEM((512, 1024), BF16),
            pltpu.VMEM((1024, 512), BF16),
            pltpu.VMEM((256, 256), BF16),
            pltpu.VMEM((6, PAD, 256), F32),
            pltpu.VMEM((6, PAD, 128), F32),
            pltpu.VMEM((6, PAD, 128), F32),
            pltpu.VMEM((2, PAD, 128), F32),
            pltpu.VMEM((3, 12, PAD, 128), F32),
            pltpu.VMEM((5, PAD, 128), F32),
            pltpu.VMEM((5, 6, PAD, 128), F32),
            pltpu.VMEM((3, 8, PAD, 128), F32),
            pltpu.VMEM((3, 8, PAD, 128), F32),
            pltpu.VMEM((8, PAD, 128), F32),
            pltpu.VMEM((8, PAD, 128), F32),
            pltpu.VMEM((6, 3, PAD, 128), F32),
            pltpu.VMEM((MPAD, 512), F32),
            pltpu.VMEM((3 * MPAD, 1024), BF16),
            pltpu.VMEM((3, 2, 128), F32),
            pltpu.VMEM((3, 2, 128), F32),
            pltpu.VMEM((3, ny, 2, 128), F32),
            pltpu.VMEM((3, nx, 2, 128), F32),
            dma((4,)),
            dma((5, 2)),
            dma((5, 2)),
            dma((5, 6)),
            dma((5, 6)),
            dma((3,)),
            dma((3,)),
            dma((3,)),
            dma((3,)),
        ],
        compiler_params=pltpu.CompilerParams(
            collective_id=0, has_side_effects=True, vmem_limit_bytes=40 << 20
        ),
        name="solve",
    )(
        innovation,
        area,
        spread_sd,
        smooth_coef.reshape(1, PLANES),
        obs_column.reshape(8, 128),
        obs_weight,
        obs_precision.reshape(8, 128),
        obs_live.reshape(8, 128),
    )
    return pl.pallas_call(
        finish,
        out_shape=[
            jax.ShapeDtypeStruct((PLANES, 16, 256), F32),
            jax.ShapeDtypeStruct((PLANES, 4, 128), F32),
        ],
        in_specs=[vmem, vmem, vmem],
        out_specs=[anywhere, vmem],
        scratch_shapes=[
            pltpu.VMEM((6, PAD, 256), F32),
            pltpu.VMEM((PAD, 16, 256), F32),
            dma((GROUPS,)),
        ],
        compiler_params=pltpu.CompilerParams(vmem_limit_bytes=24 << 20),
        name="finish",
    )(inc_low, inc_high, ctl)


def solution(mesh):
    nx, ny = mesh.shape["gx"], mesh.shape["gy"]
    return jax.shard_map(
        functools.partial(per_device, nx, ny),
        mesh=mesh,
        in_specs=(
            P(None, "gx", "gy"),
            P("gx", "gy"),
            P(None, "gx", "gy"),
            P(),
            P(("gx", "gy")),
            P(None, ("gx", "gy")),
            P(("gx", "gy")),
            P(("gx", "gy")),
        ),
        out_specs=(P(None, "gx", "gy"), P(None, "gx", "gy")),
        check_vma=False,
    )
```

time: 860 us -> 78 us (0.09); the launches traced: 844 us -> 77.6 us
  blocking collectives: 399 us -> 0 us
  starting transfers between devices: 217 us -> 0 us
  waiting for transfers between devices: 116 us -> 0 us
  Pallas kernels: 0 us -> 70.4 us
  other arithmetic: 63.1 us -> 0 us
  local copies, waits for them, and re-layouts: 39.1 us -> 6.54 us
  between operations: 9.39 us -> 0.66 us
    psum x5 -> x0, blocking collectives: 399 us -> none  [the longest x3 238 us: residual_norm(): return lax.psum(jnp.sum(resid * resid), ('gx', 'gy'))]
    ppermute x72 -> x0, starting transfers between devices: 217 us -> none  [the longest x36 153 us: extended_2(): before = lax.ppermute(last, axis, up)]
    ppermute x72 -> x0, waiting for transfers between devices: 116 us -> none  [the longest x36 97 us: extended_2(): after = lax.ppermute(leading, axis, down)]
    pallas_call x0 -> x2, Pallas kernels: none -> 70.4 us  [the longest x1 68 us: per_device(): pl.pallas_call(functools.partial(solve, nx, ny), out_shape=[jax.ShapeDtyp...]
    scatter-add x13 -> x0, other arithmetic: 48.9 us -> none  [the longest x4 22 us: spread(): middle.at[:, :, offset:offset + RY * (coarse_y - 1) + 1:RY]]
    slice x41 -> x0, local copies, waits for them, and re-layouts: 21.6 us -> none  [the longest x3 14.3 us: restrict(): along_x[:, :, offset:offset + RY * (coarse_y - 1) + 1:RY]]
  transfers between devices with their start and end apart: 72 -> 0, of which waited for: 53 -> 0; matrix products, arithmetic and copies ran while one was open for 0% -> 0% of each run, Pallas kernels for 0% -> 0%
where the time goes in v1:
time: 78 us; the launch traced here: 77.6 us
  Pallas kernels  70.4 us (90%)
  local copies, waits for them, and re-layouts  6.54 us (8%)
    pallas_call x1, Pallas kernels, per_device(): pl.pallas_call(functools.partial(solve, nx, ny), out_shape=[jax.ShapeDtyp...  68 us
    unnamed x16, local copies, waits for them, and re-layouts  6.54 us
    pallas_call x1, Pallas kernels, per_device(): pl.pallas_call(finish, out_shape=[jax.ShapeDtypeStruct((PLANES, 16, 256),...  2.41 us

profile of v1, /device:TPU:1, one launch (start us, length us, event | category | flops | bytes accessed | tf_op | source)
XLA Modules:
  0.0 77.6 jit_solution(12399017003698817200)
XLA Ops:
  0.6 0.0 copy-start
  0.6 1.2 %copy-done = f32[68,16,256]{2,1,0:T(8,128)S(1)} copy-done((f32[68,16,256]{2,1,0:T(8,128)S(1)}, f32[68,16,256]{2,1,0:T(8,128)}, u32[]{:S(2)}) %copy-start) | copy-done | bytes 1114136
  1.9 0.0 copy-start.1
  1.9 1.0 %copy-done.1 = f32[68,1024]{1,0:T(8,128)S(1)} copy-done((f32[68,1024]{1,0:T(8,128)S(1)}, f32[68,1024]{1,0:T(8,128)}, u32[]{:S(2)}) %copy-start.1) | copy-done | bytes 278552
  2.8 0.0 copy-start.2
  2.8 0.9 %copy-done.2 = f32[68,4,128]{2,1,0:T(4,128)S(1)} copy-done((f32[68,4,128]{2,1,0:T(4,128)S(1)}, f32[68,4,128]{2,1,0:T(4,128)}, u32[]{:S(2)}) %copy-start.2) | copy-done | bytes 139288
  3.8 0.0 copy-start.3
  3.8 0.7 copy-done.3
  4.5 0.0 copy-start.4
  4.5 0.7 copy-done.4
  5.2 0.0 copy-start.5
  5.2 0.7 copy-done.5
  5.8 0.0 copy-start.6
  5.8 0.7 copy-done.6
  6.5 0.0 copy-start.7
  6.5 0.7 copy-done.7
  7.2 68.0 %solve.1 = (f32[6,72,128]{2,1,0:T(8,128)S(1)}, f32[6,72,128]{2,1,0:T(8,128)S(1)}, f32[4,72,128]{2,1,0:T(8,128)S(1)}) custom-call(f32[68,16,256]{2,1,0:T(8,128)S(1)} %copy-done, f32[16,256]{1,0:T(8,128)S(1)} %copy-done.3, f32[68,4,128]{2,1,0:T(4,128)S(1)} %copy-done.2, f32[1,68]{1,0:T(1,128)S(1)} %bitcast.7, s32[8,128]{1,0:T(8,128)S(1)} %bitcast.4, ...), custom_call_target="tpu_custom_call" | custom-call | tf_op jit(solution)/shard_map/solve/pallas_call | solution.py:505
  75.2 2.4 %finish.1 = (f32[68,16,256]{2,1,0:T(8,128)}, f32[68,4,128]{2,1,0:T(4,128)}) custom-call(f32[6,72,128]{2,1,0:T(8,128)S(1)} %get-tuple-element.5.inc_low, f32[6,72,128]{2,1,0:T(8,128)S(1)} %get-tuple-element.6.inc_high, f32[4,72,128]{2,1,0:T(8,128)S(1)} %get-tuple-element.7.ctl), custom_call_target="tpu_custom_call" | custom-call | tf_op jit(solution)/shard_map/finish/pallas_call | solution.py:567
Async XLA Ops:
  0.6 1.2 %copy-start = (f32[68,16,256]{2,1,0:T(8,128)S(1)}, f32[68,16,256]{2,1,0:T(8,128)}, u32[]{:S(2)}) copy-start(f32[68,16,256]{2,1,0:T(8,128)} %inn_hbm.1) | copy-start | bytes 3342340
  1.9 1.0 %copy-start.1 = (f32[68,1024]{1,0:T(8,128)S(1)}, f32[68,1024]{1,0:T(8,128)}, u32[]{:S(2)}) copy-start(f32[68,1024]{1,0:T(8,128)} %weight_hbm.1) | copy-start | bytes 835588
  2.8 0.9 %copy-start.2 = (f32[68,4,128]{2,1,0:T(4,128)S(1)}, f32[68,4,128]{2,1,0:T(4,128)}, u32[]{:S(2)}) copy-start(f32[68,4,128]{2,1,0:T(4,128)} %sd_hbm.1) | copy-start | bytes 417796
  3.8 0.7 copy-start.3
  4.5 0.7 copy-start.4
  5.2 0.7 copy-start.5
  5.8 0.7 copy-start.6
  6.5 0.7 copy-start.7

commit v2 on v1

--- a/solution.py
+++ b/solution.py
@@ -62,11 +62,11 @@
     inn_hbm,
     area_hbm,
     sd_hbm,
-    coef_ref,
-    col_ref,
+    coef_hbm,
+    col_hbm,
     weight_hbm,
-    prec_ref,
-    live_ref,
+    prec_hbm,
+    live_hbm,
     inc_low,
     inc_high,
     ctl,
@@ -75,6 +75,10 @@
     sd_in,
     sd,
     weight,
+    coef_ref,
+    col_ref,
+    prec_ref,
+    live_ref,
     coef_a,
     coef_b,
     pick,
@@ -118,6 +122,10 @@
         pltpu.make_async_copy(area_hbm, area, in_sems.at[1]),
         pltpu.make_async_copy(sd_hbm, sd_in, in_sems.at[2]),
         pltpu.make_async_copy(weight_hbm, weight, in_sems.at[3]),
+        pltpu.make_async_copy(coef_hbm, coef_ref, in_sems.at[4]),
+        pltpu.make_async_copy(col_hbm, col_ref, in_sems.at[5]),
+        pltpu.make_async_copy(prec_hbm, prec_ref, in_sems.at[6]),
+        pltpu.make_async_copy(live_hbm, live_ref, in_sems.at[7]),
     ]
     for load in loads:
         load.start()
@@ -131,20 +139,26 @@
     lane8 = iota((8, 128), 1)
     left_ok, right_ok = gx > 0, gx < nx - 1
     low_ok, high_ok = gy > 0, gy < ny - 1
-    edge_f = jnp.where(lane8 < 64, jnp.where(high_ok, 1.0, 0.0), jnp.where(low_ok, 1.0, 0.0))
+    low_f, high_f = jnp.where(low_ok, 1.0, 0.0), jnp.where(high_ok, 1.0, 0.0)
+    edge_f = jnp.where(lane8 < 64, high_f, low_f)
     left_f, right_f = jnp.where(left_ok, 1.0, 0.0), jnp.where(right_ok, 1.0, 0.0)
+
+    def rows(g):
+        return pl.ds(8 * g, 8)
+
+    def pack(e, parts, width, block, offset):
+        per = 128 // block
+        for v in range(-(-GROUPS // per)):
+            value = jnp.zeros((8, 128), F32)
+            for g in range(per * v, min(per * v + per, GROUPS)):
+                for n, part in enumerate(parts[g]):
+                    first = block * (g % per) + width * n
+                    mine = (lane8 >= first) & (lane8 < first + width)
+                    value = jnp.where(mine, roll(part, first + offset), value)
+            packed[e, rows(v), :] = value
 
     inn[PLANES:] = jnp.zeros((PAD - PLANES, 16, 256), F32)
     gathered[PAD:] = jnp.zeros((MPAD - PAD, 512), F32)
-    diagonal = iota((PAD, PLANES), 0) == iota((PAD, PLANES), 1)
-    coef = jnp.sum(
-        jnp.where(diagonal, jnp.broadcast_to(coef_ref[...], (PAD, PLANES)), 0.0),
-        axis=1,
-        keepdims=True,
-    )
-    coef_b[...] = jnp.broadcast_to(coef, (PAD, 128))
-    coef_a[...] = jnp.broadcast_to(1.0 - 4.0 * coef, (PAD, 128))
-
     out_row, in_row = iota((48, 384), 0), iota((48, 384), 1) & 127
     same = (out_row & 7) == (in_row >> 4)
     off = (in_row & 15) - 4 * ((out_row >> 3) - 1)
@@ -166,10 +180,7 @@
     rest_low[...] = part[:, :128].reshape(6, PAD, 128)
     rest_high[...] = part[:, 128:].reshape(6, PAD, 128)
 
-    edge = jnp.zeros((PAD, 128), F32)
-    for r in range(6):
-        edge = edge + roll(rest_high[r], 1 + 2 * r)
-    packed[0] = edge
+    pack(0, [[rest_high[r, rows(g), :] for r in range(6)] for g in range(GROUPS)], 2, 16, 1)
 
     pl.semaphore_wait(barrier, len(partners))
 
@@ -188,6 +199,7 @@
     sent = []
 
     def exchange(e, to_left, at_right, to_right, at_left):
+        used = 16 if e == 0 else 24
         copies = [
             remote(to_left, at_right, x_send.at[e, 0], x_recv.at[e, 1], at(-1, 0)),
             remote(to_right, at_left, x_send.at[e, 1], x_recv.at[e, 0], at(1, 0)),
@@ -195,7 +207,11 @@
         for n, (sx, sy) in enumerate(SIDES):
             copies.append(
                 remote(
-                    packed.at[e], packed_in.at[e, n], p_send.at[e, n], p_recv.at[e, n], at(-sx, -sy)
+                    packed.at[e, pl.ds(0, used)],
+                    packed_in.at[e, n, pl.ds(0, used)],
+                    p_send.at[e, n],
+                    p_recv.at[e, n],
+                    at(-sx, -sy),
                 )
             )
         sent.extend(copies)
@@ -205,21 +221,37 @@
         for copy in copies:
             copy.wait_recv()
 
-    def sides(e, at_g, above):
+    def sides(e, count, above):
         result = []
         for sx, ok in ((-1, left_ok), (0, None), (1, right_ok)):
             n = 2 * (sx + 1)
-            both = jnp.where(above, packed_in[e, n + 1, at_g, :], packed_in[e, n, at_g, :])
-            inside = jnp.where(above, jnp.where(high_ok, 1.0, 0.0), jnp.where(low_ok, 1.0, 0.0))
+            inside = jnp.where(above, high_f, low_f)
             if ok is not None:
                 inside = inside * jnp.where(ok, 1.0, 0.0)
-            result.append(jnp.where(inside > 0.5, both, 0.0))
+            result.append(
+                [
+                    jnp.where(
+                        inside > 0.5,
+                        jnp.where(above, packed_in[e, n + 1, rows(v), :], packed_in[e, n, rows(v), :]),
+                        0.0,
+                    )
+                    for v in range(count)
+                ]
+            )
         return result
 
     copies = exchange(0, rest_low.at[0], rim_in.at[1], rest_low.at[5], rim_in.at[0])
 
-    loads[2].wait()
-    loads[3].wait()
+    for load in loads[2:]:
+        load.wait()
+    diagonal = iota((PAD, PLANES), 0) == iota((PAD, PLANES), 1)
+    coef = jnp.sum(
+        jnp.where(diagonal, jnp.broadcast_to(coef_ref[...], (PAD, PLANES)), 0.0),
+        axis=1,
+        keepdims=True,
+    )
+    coef_b[...] = jnp.broadcast_to(coef, (PAD, 128))
+    coef_a[...] = jnp.broadcast_to(1.0 - 4.0 * coef, (PAD, 128))
     for i in range(4):
         sd[i, :PLANES] = sd_in[:, i, :]
         sd[i, PLANES:] = jnp.zeros((PAD - PLANES, 128), F32)
@@ -235,37 +267,26 @@
 
     arrived(copies)
 
-    def force(g, carry):
-        at_g = pl.ds(pl.multiple_of(g * 8, 8), 8)
-        rim = sides(0, at_g, (lane8 & 1) == 0)
-        ends = (lane8 == 0) | (lane8 == 127)
+    rim = sides(0, 2, (lane8 & 1) == 0)
+    ends = (lane8 == 0) | (lane8 == 127)
+    own = [[] for g in range(GROUPS)]
+    for g in range(GROUPS):
+        v, first = g // 8, 16 * (g % 8) + 1
         for i in range(4):
-            value = rest_low[i + 1, at_g, :]
-            tails = roll(rim[1], -(2 * (i + 1) + 1))
+            value = rest_low[i + 1, rows(g), :]
+            tails = roll(rim[1][v], -(first + 2 * (i + 1)))
             if i == 0:
-                value = value + rim_in[0, at_g, :] * left_f
-                tails = tails + roll(rim[0], -11)
+                value = value + rim_in[0, rows(g), :] * left_f
+                tails = tails + roll(rim[0][v], -(first + 10))
             if i == 3:
-                value = value + rim_in[1, at_g, :] * right_f
-                tails = tails + roll(rim[2], -1)
-            value = value + jnp.where(ends, tails, 0.0)
-            field[0, 4 + i, at_g, :] = sd[i, at_g, :] * value
-        return carry
-
-    lax.fori_loop(0, GROUPS, force, 0, unroll=3)
-
-    def pack_and_send(e):
-        def pack(g, carry):
-            at_g = pl.ds(pl.multiple_of(g * 8, 8), 8)
-            value = jnp.zeros((8, 128), F32)
-            for i in range(4):
-                value = jnp.where(
-                    (lane8 >> 3) == i, roll(field[e, 4 + i, at_g, :], 4 + 8 * i), value
-                )
-            packed[1 + e, at_g, :] = value
-            return carry
-
-        lax.fori_loop(0, GROUPS, pack, 0, unroll=9)
+                value = value + rim_in[1, rows(g), :] * right_f
+                tails = tails + roll(rim[2][v], -first)
+            value = sd[i, rows(g), :] * (value + jnp.where(ends, tails, 0.0))
+            field[0, 4 + i, rows(g), :] = value
+            own[g].append(value)
+
+    def pack_and_send(e, parts):
+        pack(1 + e, parts, 8, 32, 4)
         own = field.at[e, pl.ds(4, 4)]
         return exchange(1 + e, own, field.at[e, pl.ds(8, 4)], own, field.at[e, pl.ds(0, 4)])
 
@@ -282,25 +303,26 @@
         return result
 
     def smooth_step(e, alpha, beta):
-        def step(g, norm):
-            at_g = pl.ds(pl.multiple_of(g * 8, 8), 8)
-            odd = (lane8 & 4) == 4
-            tails = sides(1 + e, at_g, odd)
-            rows = []
+        tails = sides(1 + e, 3, (lane8 & 4) == 4)
+        norm = jnp.zeros((8, 128), F32)
+        for g in range(GROUPS):
+            at_g = rows(g)
+            lines = []
             for r in range(12):
                 low = field[e, r, at_g, :]
                 if r < 4:
                     low = jnp.where(left_f > 0.5, low, 0.0)
                 if r >= 8:
                     low = jnp.where(right_f > 0.5, low, 0.0)
-                rows.append((low, roll(tails[r // 4], -(8 * (r % 4) + 4))))
+                shift = 32 * (g % 4) + 8 * (r % 4) + 4
+                lines.append((low, roll(tails[r // 4][g // 4], -shift)))
             a, b = coef_a[at_g, :], coef_b[at_g, :]
             coefs = [
                 (a * f, b * f, a * f * edge_f, b * f * edge_f) for f in (left_f, F32(1.0), right_f)
             ]
-            rows = smooth(smooth(rows, -4, coefs), -3, coefs)
+            lines = smooth(smooth(lines, -4, coefs), -3, coefs)
             values = []
-            for q, (low, high) in enumerate(rows):
+            for q, (low, high) in enumerate(lines):
                 if e > 0:
                     old_low, old_high = res_low[e - 1, q, at_g, :], res_high[e - 1, q, at_g, :]
                     low, high = low + old_low, high + old_high
@@ -321,9 +343,7 @@
                 pushed = sd[i, at_g, :] * low
                 ured[1 + i, e, at_g, :] = pushed
                 gathered[at_g, pl.ds(128 * i, 128)] = pushed
-            return norm
-
-        return lax.fori_loop(0, GROUPS, step, jnp.zeros((8, 128), F32), unroll=1)
+        return norm
 
     def observe(e, norm):
         left = pieces(gathered[...])
@@ -347,11 +367,16 @@
         msg_a[e] = jnp.concatenate([jnp.sum(norm, axis=0, keepdims=True), total], axis=0)
 
     def put_back(e):
+        own = [[] for g in range(GROUPS)]
         for h in range(2):
             value = dot(scaled[...], place[:, 256 * h : 256 * h + 256])
             value = value[:PAD] + value[MPAD : MPAD + PAD] + value[2 * MPAD : 2 * MPAD + PAD]
             for i in (2 * h, 2 * h + 1):
-                field[e, 4 + i] = sd[i] * value[:, 128 * (i % 2) : 128 * (i % 2) + 128]
+                row = sd[i] * value[:, 128 * (i % 2) : 128 * (i % 2) + 128]
+                field[e, 4 + i] = row
+                for g in range(GROUPS):
+                    own[g].append(row[8 * g : 8 * g + 8])
+        return own
 
     def reduce_start(k, msg, slots, send, recv, count, mine, partner):
         slots[k, mine] = msg[k]
@@ -388,13 +413,13 @@
         gamma = jnp.broadcast_to(total[0:1], (8, 128))
         return gamma, gamma + jnp.broadcast_to(total[1:2], (8, 128))
 
-    copies = pack_and_send(0)
+    copies = pack_and_send(0, own)
     arrived(copies)
     norm = smooth_step(0, None, None)
     observe(0, norm)
     start_a(0)
-    put_back(1)
-    copies = pack_and_send(1)
+    own = put_back(1)
+    copies = pack_and_send(1, own)
     turn(0)
     arrived(copies)
     gamma0, delta0 = end_b(0)
@@ -403,8 +428,8 @@
     norm = smooth_step(1, alpha0, None)
     observe(1, norm)
     start_a(1)
-    put_back(2)
-    copies = pack_and_send(2)
+    own = put_back(2)
+    copies = pack_and_send(2, own)
     turn(1)
     arrived(copies)
     gamma1, delta1 = end_b(1)
@@ -415,17 +440,10 @@
     observe(2, norm)
     start_a(2)
 
-    def pack_rims(g, carry):
-        at_g = pl.ds(pl.multiple_of(g * 8, 8), 8)
-        value = jnp.zeros((8, 128), F32)
-        for v in range(3):
-            for i in range(4):
-                n = 4 * v + i
-                value = jnp.where((lane8 >> 1) == n, roll(ured[1 + i, v, at_g, :], 1 + 2 * n), value)
-        packed[4, at_g, :] = value
-        return carry
-
-    lax.fori_loop(0, GROUPS, pack_rims, 0, unroll=3)
+    rims = [
+        [ured[1 + i, v, rows(g), :] for v in range(3) for i in range(4)] for g in range(GROUPS)
+    ]
+    pack(4, rims, 2, 32, 1)
     copies = exchange(4, ured.at[1], ured.at[5], ured.at[4], ured.at[0])
     turn(2)
     arrived(copies)
@@ -434,8 +452,16 @@
     alpha2 = gamma2 / (delta2 - beta2 * gamma2 / alpha1)
     parts = [alpha0 + beta1 * (alpha1 + alpha2 * beta2), alpha1 + alpha2 * beta2, alpha2]
 
-    def combine(g, carry):
-        at_g = pl.ds(pl.multiple_of(g * 8, 8), 8)
+    block = lane8 & 31
+    of_lane = jnp.where(block < 8, parts[0], jnp.where(block < 16, parts[1], parts[2]))
+    tails = []
+    for arrays in sides(4, 3, (lane8 & 1) == 1):
+        tails.append([])
+        for value in arrays:
+            value = value * of_lane
+            tails[-1].append(value + roll(value, -8) + roll(value, -16))
+    for g in range(GROUPS):
+        at_g = rows(g)
         for i in range(4):
             ctl[i, at_g, :] = (
                 parts[0] * res_low[0, 2 + i, at_g, :]
@@ -453,19 +479,9 @@
             if r == 5:
                 value = jnp.where(right_f > 0.5, value, 0.0)
             inc_low[r, at_g, :] = value
-        odd = (lane8 & 1) == 1
-        of_lane = jnp.where(lane8 < 8, parts[0], jnp.where(lane8 < 16, parts[1], parts[2]))
-        tails = []
-        for value in sides(4, at_g, odd):
-            value = value * of_lane
-            tails.append(value + roll(value, -8) + roll(value, -16))
-        for r in range(6):
-            i = (r - 1) % 4
             sx = 0 if r == 0 else 2 if r == 5 else 1
-            inc_high[r, at_g, :] = roll(tails[sx], -(2 * i + 1))
-        return carry
-
-    lax.fori_loop(0, GROUPS, combine, 0, unroll=1)
+            shift = 32 * (g % 4) + 2 * ((r - 1) % 4) + 1
+            inc_high[r, at_g, :] = roll(tails[sx][g // 4], -shift)
     for copy in sent:
         copy.wait_send()
 
@@ -509,7 +525,7 @@
             jax.ShapeDtypeStruct((6, PAD, 128), F32),
             jax.ShapeDtypeStruct((4, PAD, 128), F32),
         ],
-        in_specs=[anywhere, anywhere, anywhere, vmem, vmem, anywhere, vmem, vmem],
+        in_specs=[pl.BlockSpec(memory_space=pltpu.HBM)] * 8,
         out_specs=[vmem, vmem, vmem],
         scratch_shapes=[
             pltpu.VMEM((PAD, 16, 256), F32),
@@ -517,6 +533,10 @@
             pltpu.VMEM((PLANES, 4, 128), F32),
             pltpu.VMEM((4, PAD, 128), F32),
             pltpu.VMEM((PLANES, 1024), F32),
+            pltpu.VMEM((1, PLANES), F32),
+            pltpu.VMEM((8, 128), jnp.int32),
+            pltpu.VMEM((8, 128), F32),
+            pltpu.VMEM((8, 128), jnp.int32),
             pltpu.VMEM((PAD, 128), F32),
             pltpu.VMEM((PAD, 128), F32),
             pltpu.VMEM((512, 1024), BF16),
@@ -527,8 +547,8 @@
             pltpu.VMEM((6, PAD, 128), F32),
             pltpu.VMEM((2, PAD, 128), F32),
             pltpu.VMEM((3, 12, PAD, 128), F32),
-            pltpu.VMEM((5, PAD, 128), F32),
-            pltpu.VMEM((5, 6, PAD, 128), F32),
+            pltpu.VMEM((5, 24, 128), F32),
+            pltpu.VMEM((5, 6, 24, 128), F32),
             pltpu.VMEM((3, 8, PAD, 128), F32),
             pltpu.VMEM((3, 8, PAD, 128), F32),
             pltpu.VMEM((8, PAD, 128), F32),
@@ -540,7 +560,7 @@
             pltpu.VMEM((3, 2, 128), F32),
             pltpu.VMEM((3, ny, 2, 128), F32),
             pltpu.VMEM((3, nx, 2, 128), F32),
-            dma((4,)),
+            dma((8,)),
             dma((5, 2)),
             dma((5, 2)),
             dma((5, 6)),
@@ -555,14 +575,19 @@
         ),
         name="solve",
     )(
-        innovation,
-        area,
-        spread_sd,
-        smooth_coef.reshape(1, PLANES),
-        obs_column.reshape(8, 128),
-        obs_weight,
-        obs_precision.reshape(8, 128),
-        obs_live.reshape(8, 128),
+        *(
+            pltpu.with_memory_space_constraint(operand, pltpu.HBM)
+            for operand in (
+                innovation,
+                area,
+                spread_sd,
+                smooth_coef.reshape(1, PLANES),
+                obs_column.reshape(8, 128),
+                obs_weight,
+                obs_precision.reshape(8, 128),
+                obs_live.reshape(8, 128),
+            )
+        )
     )
     return pl.pallas_call(
         finish,

time: 78 us -> 59.4 us (0.76)
  Pallas kernels: 70.4 us -> 58.6 us
  local copies, waits for them, and re-layouts: 6.54 us -> 0 us
    pallas_call x1, Pallas kernels: 68 us -> 56.2 us  [per_device(): pl.pallas_call(functools.partial(solve, nx, ny), out_shape=[jax.ShapeDtyp...]
    unnamed x16 -> x0, local copies, waits for them, and re-layouts: 6.54 us -> none
where the time goes in v2:
time: 59.4 us; the launch traced here: 59.3 us
  Pallas kernels  58.6 us (99%)
  between operations  0.64 us (1%)
    pallas_call x1, Pallas kernels, per_device(): pl.pallas_call(functools.partial(solve, nx, ny), out_shape=[jax.ShapeDtyp...  56.2 us
    pallas_call x1, Pallas kernels, per_device(): pl.pallas_call(finish, out_shape=[jax.ShapeDtypeStruct((PLANES, 16, 256),...  2.41 us

profile of v2, /device:TPU:1, one launch (start us, length us, event | category | flops | bytes accessed | tf_op | source)
XLA Modules:
  0.0 59.3 jit_solution(5771748747853390028)
XLA Ops:
  0.6 56.2 %solve.1 = (f32[6,72,128]{2,1,0:T(8,128)S(1)}, f32[6,72,128]{2,1,0:T(8,128)S(1)}, f32[4,72,128]{2,1,0:T(8,128)S(1)}) custom-call(f32[68,16,256]{2,1,0:T(8,128)} %inn_hbm.1, f32[16,256]{1,0:T(8,128)} %area_hbm.1, f32[68,4,128]{2,1,0:T(4,128)} %sd_hbm.1, f32[1,68]{1,0:T(1,128)} %bitcast.7, s32[8,128]{1,0:T(8,128)} %bitcast.4, f32[68,1024]{1,0:T(8,128)} %weight_hbm.1, ...), custom_call_target="tpu_custom_call" | custom-call | tf_op jit(solution)/shard_map/solve/pallas_call | solution.py:521
  56.9 2.4 %finish.1 = (f32[68,16,256]{2,1,0:T(8,128)}, f32[68,4,128]{2,1,0:T(4,128)}) custom-call(f32[6,72,128]{2,1,0:T(8,128)S(1)} %get-tuple-element.5.inc_low, f32[6,72,128]{2,1,0:T(8,128)S(1)} %get-tuple-element.6.inc_high, f32[4,72,128]{2,1,0:T(8,128)S(1)} %get-tuple-element.7.ctl), custom_call_target="tpu_custom_call" | custom-call | tf_op jit(solution)/shard_map/finish/pallas_call | solution.py:592

commit v3 on v2

--- a/solution.py
+++ b/solution.py
@@ -67,9 +67,9 @@
     weight_hbm,
     prec_hbm,
     live_hbm,
-    inc_low,
-    inc_high,
+    fine,
     ctl,
+    steps,
     inn,
     area,
     sd_in,
@@ -91,10 +91,8 @@
     field,
     packed,
     packed_in,
-    res_low,
-    res_high,
-    dir_low,
-    dir_high,
+    base_low,
+    base_high,
     ured,
     gathered,
     scaled,
@@ -114,8 +112,15 @@
 ):
     gx, gy = lax.axis_index("gx"), lax.axis_index("gy")
 
+    def shifted(here, step, size):
+        if step == 0:
+            return here
+        if size & (size - 1) == 0:
+            return (here + (step + size)) & (size - 1)
+        return lax.rem(here + (step + size), size)
+
     def at(dx, dy):
-        return (lax.rem(gx + dx + nx, nx), lax.rem(gy + dy + ny, ny))
+        return (shifted(gx, dx, nx), shifted(gy, dy, ny))
 
     loads = [
         pltpu.make_async_copy(inn_hbm, inn.at[pl.ds(0, PLANES)], in_sems.at[0]),
@@ -198,40 +203,68 @@
 
     sent = []
 
-    def exchange(e, to_left, at_right, to_right, at_left):
-        used = 16 if e == 0 else 24
-        copies = [
-            remote(to_left, at_right, x_send.at[e, 0], x_recv.at[e, 1], at(-1, 0)),
-            remote(to_right, at_left, x_send.at[e, 1], x_recv.at[e, 0], at(1, 0)),
-        ]
-        for n, (sx, sy) in enumerate(SIDES):
-            copies.append(
-                remote(
-                    packed.at[e, pl.ds(0, used)],
-                    packed_in.at[e, n, pl.ds(0, used)],
-                    p_send.at[e, n],
-                    p_recv.at[e, n],
-                    at(-sx, -sy),
-                )
+    def inside(dx, dy):
+        ok = None
+        for here, step, size in ((gx, dx, nx), (gy, dy, ny)):
+            if step:
+                holds = here > 0 if step < 0 else here < size - 1
+                ok = holds if ok is None else ok & holds
+        return ok
+
+    def send(moves):
+        copies = []
+        for dx, dy, source, target, send_sem, recv_sem in moves:
+            copy = pltpu.make_async_remote_copy(
+                src_ref=source,
+                dst_ref=target,
+                send_sem=send_sem,
+                recv_sem=recv_sem,
+                device_id=at(dx, dy),
+                device_id_type=MESH,
             )
+            pl.when(inside(dx, dy))(copy.start)
+            copies.append((dx, dy, copy))
         sent.extend(copies)
         return copies
 
+    def row_moves(e, to_left, at_right, to_right, at_left):
+        return [
+            (-1, 0, to_left, at_right, x_send.at[e, 0], x_recv.at[e, 1]),
+            (1, 0, to_right, at_left, x_send.at[e, 1], x_recv.at[e, 0]),
+        ]
+
+    def side_moves(e):
+        used = pl.ds(0, 16 if e == 0 else 24)
+        return [
+            (
+                -sx,
+                -sy,
+                packed.at[e, used],
+                packed_in.at[e, n, used],
+                p_send.at[e, n],
+                p_recv.at[e, n],
+            )
+            for n, (sx, sy) in enumerate(SIDES)
+        ]
+
+    def rim_rows(v):
+        return row_moves(4 + v, ured.at[1, v], ured.at[5, v], ured.at[4, v], ured.at[0, v])
+
     def arrived(copies):
-        for copy in copies:
-            copy.wait_recv()
+        for dx, dy, copy in copies:
+            pl.when(inside(-dx, -dy))(copy.wait_recv)
 
     def sides(e, count, above):
         result = []
         for sx, ok in ((-1, left_ok), (0, None), (1, right_ok)):
             n = 2 * (sx + 1)
-            inside = jnp.where(above, high_f, low_f)
+            there = jnp.where(above, high_f, low_f)
             if ok is not None:
-                inside = inside * jnp.where(ok, 1.0, 0.0)
+                there = there * jnp.where(ok, 1.0, 0.0)
             result.append(
                 [
                     jnp.where(
-                        inside > 0.5,
+                        there > 0.5,
                         jnp.where(above, packed_in[e, n + 1, rows(v), :], packed_in[e, n, rows(v), :]),
                         0.0,
                     )
@@ -240,7 +273,9 @@
             )
         return result
 
-    copies = exchange(0, rest_low.at[0], rim_in.at[1], rest_low.at[5], rim_in.at[0])
+    copies = send(
+        row_moves(0, rest_low.at[0], rim_in.at[1], rest_low.at[5], rim_in.at[0]) + side_moves(0)
+    )
 
     for load in loads[2:]:
         load.wait()
@@ -276,10 +311,10 @@
             value = rest_low[i + 1, rows(g), :]
             tails = roll(rim[1][v], -(first + 2 * (i + 1)))
             if i == 0:
-                value = value + rim_in[0, rows(g), :] * left_f
+                value = value + jnp.where(left_f > 0.5, rim_in[0, rows(g), :], 0.0)
                 tails = tails + roll(rim[0][v], -(first + 10))
             if i == 3:
-                value = value + rim_in[1, rows(g), :] * right_f
+                value = value + jnp.where(right_f > 0.5, rim_in[1, rows(g), :], 0.0)
                 tails = tails + roll(rim[2][v], -first)
             value = sd[i, rows(g), :] * (value + jnp.where(ends, tails, 0.0))
             field[0, 4 + i, rows(g), :] = value
@@ -288,7 +323,8 @@
     def pack_and_send(e, parts):
         pack(1 + e, parts, 8, 32, 4)
         own = field.at[e, pl.ds(4, 4)]
-        return exchange(1 + e, own, field.at[e, pl.ds(8, 4)], own, field.at[e, pl.ds(0, 4)])
+        after, before = field.at[e, pl.ds(8, 4)], field.at[e, pl.ds(0, 4)]
+        return send(row_moves(1 + e, own, after, own, before) + side_moves(1 + e))
 
     def smooth(rows, first, coefs):
         result = []
@@ -302,9 +338,8 @@
             result.append((a * low + b * of_low, a_high * high + b_high * of_high))
         return result
 
-    def smooth_step(e, alpha, beta):
+    def smooth_step(e, alpha):
         tails = sides(1 + e, 3, (lane8 & 4) == 4)
-        norm = jnp.zeros((8, 128), F32)
         for g in range(GROUPS):
             at_g = rows(g)
             lines = []
@@ -324,47 +359,62 @@
             values = []
             for q, (low, high) in enumerate(lines):
                 if e > 0:
-                    old_low, old_high = res_low[e - 1, q, at_g, :], res_high[e - 1, q, at_g, :]
-                    low, high = low + old_low, high + old_high
-                    if e > 1:
-                        low = low + beta * dir_low[q, at_g, :]
-                        high = high + beta * dir_high[q, at_g, :]
-                    else:
-                        dir_low[q, at_g, :] = low
-                        dir_high[q, at_g, :] = high
-                    low, high = old_low - alpha * low, old_high - alpha * high
-                res_low[e, q, at_g, :] = low
-                res_high[e, q, at_g, :] = high
+                    low, high = low + base_low[0, q, at_g, :], high + base_high[0, q, at_g, :]
+                if e > 1:
+                    low = low - alpha * base_low[1, q, at_g, :]
+                    high = high - alpha * base_high[1, q, at_g, :]
+                base_low[e, q, at_g, :] = low
+                if e < 2:
+                    base_high[e, q, at_g, :] = high
                 values.append((low, high))
-                if 2 <= q < 6:
-                    norm = norm + low * low
             values = smooth(smooth(values, -2, coefs), -1, coefs)
             for i, (low, _) in enumerate(values):
                 pushed = sd[i, at_g, :] * low
                 ured[1 + i, e, at_g, :] = pushed
                 gathered[at_g, pl.ds(128 * i, 128)] = pushed
-        return norm
-
-    def observe(e, norm):
+
+    def observe():
         left = pieces(gathered[...])
-        total = jnp.zeros((1, 128), F32)
-        live = iota((PLANES, 256), 0) >= 0
+        seen = []
         for n in range(4):
             k = pl.ds(256 * n, 256)
             taken = dot(left, pick[:, k])
             taken = taken[:MPAD] + taken[MPAD : 2 * MPAD] + taken[2 * MPAD :]
-            w = weight[:, k]
-            seen = jnp.sum(w * taken[:PLANES], axis=0, keepdims=True)
+            seen.append(jnp.sum(weight[:, k] * taken[:PLANES], axis=0, keepdims=True))
+        return seen
+
+    def wide(x):
+        return jnp.concatenate([x[:1], x[:1]], axis=1)
+
+    def squares(e, seen, norm):
+        scaled_seen, total = [], jnp.zeros((1, 128), F32)
+        for n in range(4):
             scale = jnp.concatenate(
                 [obs_scale[2 * n : 2 * n + 1], obs_scale[2 * n + 1 : 2 * n + 2]], axis=1
             )
-            value = scale * seen
-            square = value * seen
+            value = scale * seen[n]
+            scaled_seen.append(value)
+            square = value * seen[n]
             total = total + square[:, :128] + square[:, 128:]
-            if e < 2:
-                back = jnp.concatenate([w * value, jnp.zeros((MPAD - PLANES, 256), F32)], axis=0)
-                scaled[:, k] = pieces(back)
         msg_a[e] = jnp.concatenate([jnp.sum(norm, axis=0, keepdims=True), total], axis=0)
+        return scaled_seen
+
+    def scatter(scaled_seen):
+        for n in range(4):
+            k = pl.ds(256 * n, 256)
+            back = weight[:, k] * scaled_seen[n]
+            back = jnp.concatenate([back, jnp.zeros((MPAD - PLANES, 256), F32)], axis=0)
+            scaled[:, k] = pieces(back)
+
+    def own_norm(factors):
+        norm = jnp.zeros((8, 128), F32)
+        for g in range(GROUPS):
+            for i in range(4):
+                value = base_low[0, 2 + i, rows(g), :]
+                for v, factor in enumerate(factors):
+                    value = value + factor * base_low[1 + v, 2 + i, rows(g), :]
+                norm = norm + value * value
+        return norm
 
     def put_back(e):
         own = [[] for g in range(GROUPS)]
@@ -378,137 +428,188 @@
                     own[g].append(row[8 * g : 8 * g + 8])
         return own
 
-    def reduce_start(k, msg, slots, send, recv, count, mine, partner):
+    def reduce_start(k, msg, slots, send_sem, recv_sem, offsets, mine, partner):
         slots[k, mine] = msg[k]
-        for o in range(1, count):
-            remote(msg.at[k], slots.at[k, mine], send.at[k], recv.at[k], partner(o))
-
-    def reduce_end(k, slots, send, recv, count, partner):
+        for o in offsets:
+            pltpu.make_async_remote_copy(
+                src_ref=msg.at[k],
+                dst_ref=slots.at[k, mine],
+                send_sem=send_sem.at[k],
+                recv_sem=recv_sem.at[k],
+                device_id=partner(o),
+                device_id_type=MESH,
+            ).start()
+
+    def all_of(k, slots, send_sem, recv_sem, count, partner):
         several = slots.at[k, pl.ds(0, count - 1)]
-        whole = pltpu.make_async_remote_copy(
+        return pltpu.make_async_remote_copy(
             src_ref=several,
             dst_ref=several,
-            send_sem=send.at[k],
-            recv_sem=recv.at[k],
+            send_sem=send_sem.at[k],
+            recv_sem=recv_sem.at[k],
             device_id=partner(1),
             device_id_type=MESH,
         )
-        whole.wait_recv()
-        whole.wait_send()
-        total = slots[k, 0]
-        for o in range(1, count):
-            total = total + slots[k, o]
-        return total
+
+    def total_of(k, slots, count):
+        totals = [slots[k, o] for o in range(count)]
+        while len(totals) > 1:
+            totals = [sum(totals[n : n + 2]) for n in range(0, len(totals), 2)]
+        return totals[0]
+
+    def far_first(size):
+        return sorted(range(1, size), key=lambda o: -min(o, size - o))
+
+    def over_y(o):
+        return at(0, o)
+
+    def over_x(o):
+        return at(o, 0)
 
     def start_a(k):
-        reduce_start(k, msg_a, slots_a, a_send, a_recv, ny, gy, lambda o: at(0, o))
+        reduce_start(k, msg_a, slots_a, a_send, a_recv, far_first(ny), gy, over_y)
 
     def turn(k):
-        msg_b[k] = reduce_end(k, slots_a, a_send, a_recv, ny, lambda o: at(0, o))
-        reduce_start(k, msg_b, slots_b, b_send, b_recv, nx, gx, lambda o: at(o, 0))
+        all_of(k, slots_a, a_send, a_recv, ny, over_y).wait_recv()
+        msg_b[k] = total_of(k, slots_a, ny)
+        reduce_start(k, msg_b, slots_b, b_send, b_recv, far_first(nx), gx, over_x)
 
     def end_b(k):
-        total = reduce_end(k, slots_b, b_send, b_recv, nx, lambda o: at(o, 0))
+        all_of(k, slots_b, b_send, b_recv, nx, over_x).wait_recv()
+        total = total_of(k, slots_b, nx)
         total = jnp.sum(total, axis=1, keepdims=True)
         gamma = jnp.broadcast_to(total[0:1], (8, 128))
         return gamma, gamma + jnp.broadcast_to(total[1:2], (8, 128))
 
     copies = pack_and_send(0, own)
     arrived(copies)
-    norm = smooth_step(0, None, None)
-    observe(0, norm)
+    smooth_step(0, None)
+    seen0 = observe()
+    values = squares(0, seen0, own_norm([]))
     start_a(0)
+    scatter(values)
     own = put_back(1)
     copies = pack_and_send(1, own)
     turn(0)
     arrived(copies)
+
+    rims = send(rim_rows(0))
+    smooth_step(1, None)
+    seen1 = observe()
     gamma0, delta0 = end_b(0)
     alpha0 = gamma0 / delta0
-
-    norm = smooth_step(1, alpha0, None)
-    observe(1, norm)
+    seen_r1 = [a - wide(alpha0) * b for a, b in zip(seen0, seen1)]
+    values = squares(1, seen_r1, own_norm([-alpha0]))
     start_a(1)
+    scatter(values)
     own = put_back(2)
     copies = pack_and_send(2, own)
     turn(1)
     arrived(copies)
+
+    rims += send(rim_rows(1))
+    smooth_step(2, alpha0)
+    edges = [
+        [ured[1 + i, v, rows(g), :] for v in range(3) for i in range(4)] for g in range(GROUPS)
+    ]
+    pack(4, edges, 2, 32, 1)
+    rims += send(rim_rows(2) + side_moves(4))
+    seen2 = observe()
     gamma1, delta1 = end_b(1)
     beta1 = gamma1 / gamma0
     alpha1 = gamma1 / (delta1 - beta1 * gamma1 / alpha0)
-
-    norm = smooth_step(2, alpha1, beta1)
-    observe(2, norm)
+    seen_r2 = [
+        a - wide(alpha1) * (b + wide(beta1) * c) for a, b, c in zip(seen_r1, seen2, seen1)
+    ]
+    of_r2 = [-alpha0 - alpha1 * beta1, -alpha1]
+    squares(2, seen_r2, own_norm(of_r2))
     start_a(2)
 
-    rims = [
-        [ured[1 + i, v, rows(g), :] for v in range(3) for i in range(4)] for g in range(GROUPS)
+    both = 1.0 + beta1
+    factors = [
+        [alpha0 + alpha1 * both, -alpha1 * alpha0],
+        [jnp.ones((8, 128), F32)] + of_r2,
+        [both, -alpha0],
     ]
-    pack(4, rims, 2, 32, 1)
-    copies = exchange(4, ured.at[1], ured.at[5], ured.at[4], ured.at[0])
+    for g in range(GROUPS):
+        for i in range(4):
+            for b in range(3):
+                ctl[b, i, rows(g), :] = sum(
+                    f * base_low[v, 2 + i, rows(g), :] for v, f in enumerate(factors[b])
+                )
+    arrived(rims)
+    tails = sides(4, 3, (lane8 & 1) == 1)
+    block = lane8 & 31
+    out_row, in_col = iota((128, 48), 0), iota((128, 48), 1)
+    off = (out_row & 15) - 4 * ((in_col >> 3) - 1)
+    spread_x = jnp.where((in_col & 7) == (out_row >> 4), tap(off, 4), 0.0).astype(BF16)
+    spread_x = jnp.concatenate([spread_x] * 3, axis=1)
+    spread_y = tap(iota((256, 256), 1) - 2 * coarse_lane(iota((256, 256), 0)), 2).astype(BF16)
+    sides_in = (lane8 == 0) | (lane8 == 127)
+
+    def interpolate(b):
+        most = factors[b] + [jnp.zeros((8, 128), F32)] * (3 - len(factors[b]))
+        of_lane = jnp.where(block < 8, most[0], jnp.where(block < 16, most[1], most[2]))
+        ends = []
+        for arrays in tails:
+            ends.append([])
+            for value in arrays:
+                value = value * of_lane
+                ends[-1].append(value + roll(value, -8) + roll(value, -16))
+        for g in range(GROUPS):
+            for r in range(6):
+                value = sum(f * ured[r, v, rows(g), :] for v, f in enumerate(factors[b]))
+                if r == 0:
+                    value = jnp.where(left_f > 0.5, value, 0.0)
+                if r == 5:
+                    value = jnp.where(right_f > 0.5, value, 0.0)
+                sx = 0 if r == 0 else 2 if r == 5 else 1
+                shift = 32 * (g % 4) + 2 * ((r - 1) % 4) + 1
+                end = jnp.where(sides_in, roll(ends[sx][g // 4], -shift), 0.0)
+                along[r, rows(g), :] = jnp.concatenate([value, end], axis=1)
+        out = dot(pieces(along[...].reshape(6 * PAD, 256)), spread_y)
+        out = (out[: 6 * PAD] + out[6 * PAD : 12 * PAD] + out[12 * PAD :]) * (1.0 / 60.0)
+        out = out.reshape(6, PAD, 256)
+        for g in range(GROUPS):
+            part = dot(spread_x, pieces(out[:, 8 * g : 8 * g + 8, :].reshape(48, 256)))
+            fine[b, rows(g)] = part.reshape(8, 16, 256)
+
+    interpolate(0)
     turn(2)
-    arrived(copies)
+    interpolate(1)
+    interpolate(2)
     gamma2, delta2 = end_b(2)
     beta2 = gamma2 / gamma1
     alpha2 = gamma2 / (delta2 - beta2 * gamma2 / alpha1)
-    parts = [alpha0 + beta1 * (alpha1 + alpha2 * beta2), alpha1 + alpha2 * beta2, alpha2]
-
-    block = lane8 & 31
-    of_lane = jnp.where(block < 8, parts[0], jnp.where(block < 16, parts[1], parts[2]))
-    tails = []
-    for arrays in sides(4, 3, (lane8 & 1) == 1):
-        tails.append([])
-        for value in arrays:
-            value = value * of_lane
-            tails[-1].append(value + roll(value, -8) + roll(value, -16))
-    for g in range(GROUPS):
-        at_g = rows(g)
-        for i in range(4):
-            ctl[i, at_g, :] = (
-                parts[0] * res_low[0, 2 + i, at_g, :]
-                + parts[1] * res_low[1, 2 + i, at_g, :]
-                + parts[2] * res_low[2, 2 + i, at_g, :]
-            )
-        for r in range(6):
-            value = (
-                parts[0] * ured[r, 0, at_g, :]
-                + parts[1] * ured[r, 1, at_g, :]
-                + parts[2] * ured[r, 2, at_g, :]
-            )
-            if r == 0:
-                value = jnp.where(left_f > 0.5, value, 0.0)
-            if r == 5:
-                value = jnp.where(right_f > 0.5, value, 0.0)
-            inc_low[r, at_g, :] = value
-            sx = 0 if r == 0 else 2 if r == 5 else 1
-            shift = 32 * (g % 4) + 2 * ((r - 1) % 4) + 1
-            inc_high[r, at_g, :] = roll(tails[sx][g // 4], -shift)
-    for copy in sent:
-        copy.wait_send()
-
-
-def finish(inc_low, inc_high, ctl, fine_hbm, control, along, fine, sems):
-    lane, row = iota((256, 256), 0), iota((256, 256), 1)
-    taps_y = tap(row - 2 * coarse_lane(lane), 2).astype(BF16)
-    low, high = inc_low[...].reshape(6 * PAD, 128), inc_high[...].reshape(6 * PAD, 128)
-    high = jnp.where((iota(high.shape, 1) == 0) | (iota(high.shape, 1) == 127), high, 0.0)
-    wide = dot(pieces(jnp.concatenate([low, high], axis=1)), taps_y)
-    wide = (wide[: 6 * PAD] + wide[6 * PAD : 12 * PAD] + wide[12 * PAD :]) * (1.0 / 60.0)
-    along[...] = wide.reshape(6, PAD, 256)
-
-    out_row, n = iota((128, 48), 0), iota((128, 48), 1)
-    off = (out_row & 15) - 4 * ((n >> 3) - 1)
-    taps_x = jnp.where((n & 7) == (out_row >> 4), tap(off, 4), 0.0).astype(BF16)
-    taps_x = jnp.concatenate([taps_x] * 3, axis=1)
+    steps[0] = alpha2
+    steps[1] = alpha2 * beta2
+
+    for dx, dy, copy in sent:
+        pl.when(inside(dx, dy))(copy.wait_send)
+    for k in range(3):
+        all_of(k, slots_a, a_send, a_recv, ny, over_y).wait_send()
+        all_of(k, slots_b, b_send, b_recv, nx, over_x).wait_send()
+
+
+def finish(parts, ctl, steps, fine_hbm, control, fine, sems):
+    first, second = steps[0], steps[1]
+    first = jnp.concatenate([first, first], axis=1)
+    second = jnp.concatenate([second, second], axis=1)
     copies = []
     for g in range(GROUPS):
         count = min(8, PLANES - 8 * g)
-        block = dot(taps_x, pieces(along[:, 8 * g : 8 * g + 8, :].reshape(48, 256)))
-        fine[8 * g : 8 * g + 8] = block.reshape(8, 16, 256)
+        for p in range(8 * g, 8 * g + count):
+            for h in range(2):
+                at_h = pl.ds(8 * h, 8)
+                fine[p, at_h, :] = (
+                    parts[0, p, at_h, :] + first * parts[1, p, at_h, :] + second * parts[2, p, at_h, :]
+                )
         planes = pl.ds(8 * g, count)
         copies.append(pltpu.make_async_copy(fine.at[planes], fine_hbm.at[planes], sems.at[g]))
         copies[-1].start()
     for i in range(4):
-        control[:, i, :] = ctl[i, :PLANES, :]
+        value = ctl[0, i] + steps[0][:1] * ctl[1, i] + steps[1][:1] * ctl[2, i]
+        control[:, i, :] = value[:PLANES]
     for copy in copies:
         copy.wait()
 
@@ -518,12 +619,12 @@
 ):
     vmem, anywhere = pl.BlockSpec(memory_space=pltpu.VMEM), pl.BlockSpec(memory_space=pl.ANY)
     dma = pltpu.SemaphoreType.DMA
-    inc_low, inc_high, ctl = pl.pallas_call(
+    fine, ctl, steps = pl.pallas_call(
         functools.partial(solve, nx, ny),
         out_shape=[
-            jax.ShapeDtypeStruct((6, PAD, 128), F32),
-            jax.ShapeDtypeStruct((6, PAD, 128), F32),
-            jax.ShapeDtypeStruct((4, PAD, 128), F32),
+            jax.ShapeDtypeStruct((3, PAD, 16, 256), F32),
+            jax.ShapeDtypeStruct((3, 4, PAD, 128), F32),
+            jax.ShapeDtypeStruct((2, 8, 128), F32),
         ],
         in_specs=[pl.BlockSpec(memory_space=pltpu.HBM)] * 8,
         out_specs=[vmem, vmem, vmem],
@@ -550,9 +651,7 @@
             pltpu.VMEM((5, 24, 128), F32),
             pltpu.VMEM((5, 6, 24, 128), F32),
             pltpu.VMEM((3, 8, PAD, 128), F32),
-            pltpu.VMEM((3, 8, PAD, 128), F32),
-            pltpu.VMEM((8, PAD, 128), F32),
-            pltpu.VMEM((8, PAD, 128), F32),
+            pltpu.VMEM((2, 8, PAD, 128), F32),
             pltpu.VMEM((6, 3, PAD, 128), F32),
             pltpu.VMEM((MPAD, 512), F32),
             pltpu.VMEM((3 * MPAD, 1024), BF16),
@@ -561,8 +660,8 @@
             pltpu.VMEM((3, ny, 2, 128), F32),
             pltpu.VMEM((3, nx, 2, 128), F32),
             dma((8,)),
-            dma((5, 2)),
-            dma((5, 2)),
+            dma((7, 2)),
+            dma((7, 2)),
             dma((5, 6)),
             dma((5, 6)),
             dma((3,)),
@@ -598,13 +697,12 @@
         in_specs=[vmem, vmem, vmem],
         out_specs=[anywhere, vmem],
         scratch_shapes=[
-            pltpu.VMEM((6, PAD, 256), F32),
             pltpu.VMEM((PAD, 16, 256), F32),
             dma((GROUPS,)),
         ],
         compiler_params=pltpu.CompilerParams(vmem_limit_bytes=24 << 20),
         name="finish",
-    )(inc_low, inc_high, ctl)
+    )(fine, ctl, steps)
 
 
 def solution(mesh):

time: 59.4 us -> 54.6 us (0.919)
  Pallas kernels: 58.6 us -> 53.9 us
    pallas_call x1, Pallas kernels: 56.2 us -> 52.2 us  [per_device(): pl.pallas_call(functools.partial(solve, nx, ny), out_shape=[jax.ShapeDtyp...]
    pallas_call x1, Pallas kernels: 2.41 us -> 1.73 us  [per_device(): pl.pallas_call(finish, out_shape=[jax.ShapeDtypeStruct((PLANES, 16, 256),...]
where the time goes in v3:
time: 54.6 us; the launch traced here: 54.5 us
  Pallas kernels  53.9 us (99%)
  between operations  0.64 us (1%)
    pallas_call x1, Pallas kernels, per_device(): pl.pallas_call(functools.partial(solve, nx, ny), out_shape=[jax.ShapeDtyp...  52.2 us
    pallas_call x1, Pallas kernels, per_device(): pl.pallas_call(finish, out_shape=[jax.ShapeDtypeStruct((PLANES, 16, 256),...  1.73 us

profile of v3, /device:TPU:1, one launch (start us, length us, event | category | flops | bytes accessed | tf_op | source)
XLA Modules:
  0.0 54.5 jit_solution(15097769759098054641)
XLA Ops:
  0.6 52.2 %solve.1 = (f32[3,72,16,256]{3,2,1,0:T(8,128)S(1)}, f32[3,4,72,128]{3,2,1,0:T(8,128)S(1)}, f32[2,8,128]{2,1,0:T(8,128)S(1)}) custom-call(f32[68,16,256]{2,1,0:T(8,128)} %inn_hbm.1, f32[16,256]{1,0:T(8,128)} %area_hbm.1, f32[68,4,128]{2,1,0:T(4,128)} %sd_hbm.1, f32[1,68]{1,0:T(1,128)} %bitcast.7, s32[8,128]{1,0:T(8,128)} %bitcast.4, f32[68,1024]{1,0:T(8,128)} %weight_hbm.1, ...), custom_call_target="tpu_custom_call" | custom-call | tf_op jit(solution)/shard_map/solve/pallas_call | solution.py:622
  52.8 1.7 %finish.1 = (f32[68,16,256]{2,1,0:T(8,128)}, f32[68,4,128]{2,1,0:T(4,128)}) custom-call(f32[3,72,16,256]{3,2,1,0:T(8,128)S(1)} %get-tuple-element.5.parts, f32[3,4,72,128]{3,2,1,0:T(8,128)S(1)} %get-tuple-element.6.ctl, f32[2,8,128]{2,1,0:T(8,128)S(1)} %get-tuple-element.7.steps), custom_call_target="tpu_custom_call" | custom-call | tf_op jit(solution)/shard_map/finish/pallas_call | solution.py:691

commit v4 on v3

--- a/solution.py
+++ b/solution.py
@@ -14,6 +14,8 @@
 PAD = 72
 MPAD = 80
 GROUPS = PAD // 8
+SCALE = 1.0 / 256.0
+PAIRS = [(0, 0), (0, 1), (0, 2), (1, 1), (1, 2), (2, 2)]
 SIDES = [(sx, sy) for sx in (-1, 0, 1) for sy in (-1, 1)]
 
 
@@ -91,8 +93,7 @@
     field,
     packed,
     packed_in,
-    base_low,
-    base_high,
+    base,
     ured,
     gathered,
     scaled,
@@ -244,7 +245,7 @@
                 p_send.at[e, n],
                 p_recv.at[e, n],
             )
-            for n, (sx, sy) in enumerate(SIDES)
+            for n, (sx, sy) in sorted(enumerate(SIDES), key=lambda side: -abs(side[1][0]))
         ]
 
     def rim_rows(v):
@@ -274,7 +275,7 @@
         return result
 
     copies = send(
-        row_moves(0, rest_low.at[0], rim_in.at[1], rest_low.at[5], rim_in.at[0]) + side_moves(0)
+        side_moves(0) + row_moves(0, rest_low.at[0], rim_in.at[1], rest_low.at[5], rim_in.at[0])
     )
 
     for load in loads[2:]:
@@ -299,6 +300,10 @@
         of_slot = jnp.broadcast_to(cols_t[:, a : a + 1], (128, 512))
         place[k, :] = jnp.where(of_slot == iota((128, 512), 1).astype(F32), 1.0, 0.0).astype(BF16)
     obs_scale = prec_ref[...] * live_ref[...].astype(F32)
+    scale = [
+        jnp.concatenate([obs_scale[2 * n : 2 * n + 1], obs_scale[2 * n + 1 : 2 * n + 2]], axis=1)
+        for n in range(4)
+    ]
 
     arrived(copies)
 
@@ -324,7 +329,7 @@
         pack(1 + e, parts, 8, 32, 4)
         own = field.at[e, pl.ds(4, 4)]
         after, before = field.at[e, pl.ds(8, 4)], field.at[e, pl.ds(0, 4)]
-        return send(row_moves(1 + e, own, after, own, before) + side_moves(1 + e))
+        return send(side_moves(1 + e) + row_moves(1 + e, own, after, own, before))
 
     def smooth(rows, first, coefs):
         result = []
@@ -338,7 +343,7 @@
             result.append((a * low + b * of_low, a_high * high + b_high * of_high))
         return result
 
-    def smooth_step(e, alpha):
+    def smooth_step(e):
         tails = sides(1 + e, 3, (lane8 & 4) == 4)
         for g in range(GROUPS):
             at_g = rows(g)
@@ -356,18 +361,9 @@
                 (a * f, b * f, a * f * edge_f, b * f * edge_f) for f in (left_f, F32(1.0), right_f)
             ]
             lines = smooth(smooth(lines, -4, coefs), -3, coefs)
-            values = []
-            for q, (low, high) in enumerate(lines):
-                if e > 0:
-                    low, high = low + base_low[0, q, at_g, :], high + base_high[0, q, at_g, :]
-                if e > 1:
-                    low = low - alpha * base_low[1, q, at_g, :]
-                    high = high - alpha * base_high[1, q, at_g, :]
-                base_low[e, q, at_g, :] = low
-                if e < 2:
-                    base_high[e, q, at_g, :] = high
-                values.append((low, high))
-            values = smooth(smooth(values, -2, coefs), -1, coefs)
+            for i in range(4):
+                base[e, i, at_g, :] = lines[2 + i][0]
+            values = smooth(smooth(lines, -2, coefs), -1, coefs)
             for i, (low, _) in enumerate(values):
                 pushed = sd[i, at_g, :] * low
                 ured[1 + i, e, at_g, :] = pushed
@@ -383,38 +379,32 @@
             seen.append(jnp.sum(weight[:, k] * taken[:PLANES], axis=0, keepdims=True))
         return seen
 
-    def wide(x):
-        return jnp.concatenate([x[:1], x[:1]], axis=1)
-
-    def squares(e, seen, norm):
-        scaled_seen, total = [], jnp.zeros((1, 128), F32)
-        for n in range(4):
-            scale = jnp.concatenate(
-                [obs_scale[2 * n : 2 * n + 1], obs_scale[2 * n + 1 : 2 * n + 2]], axis=1
-            )
-            value = scale * seen[n]
-            scaled_seen.append(value)
-            square = value * seen[n]
-            total = total + square[:, :128] + square[:, 128:]
-        msg_a[e] = jnp.concatenate([jnp.sum(norm, axis=0, keepdims=True), total], axis=0)
-        return scaled_seen
-
-    def scatter(scaled_seen):
+    def scatter(seen):
         for n in range(4):
             k = pl.ds(256 * n, 256)
-            back = weight[:, k] * scaled_seen[n]
+            back = weight[:, k] * (seen[n] * scale[n] * SCALE)
             back = jnp.concatenate([back, jnp.zeros((MPAD - PLANES, 256), F32)], axis=0)
             scaled[:, k] = pieces(back)
 
-    def own_norm(factors):
-        norm = jnp.zeros((8, 128), F32)
-        for g in range(GROUPS):
-            for i in range(4):
-                value = base_low[0, 2 + i, rows(g), :]
-                for v, factor in enumerate(factors):
-                    value = value + factor * base_low[1 + v, 2 + i, rows(g), :]
-                norm = norm + value * value
-        return norm
+    def products(seen):
+        parts = []
+        for i, j in PAIRS:
+            total = jnp.zeros((8, 128), F32)
+            for g in range(GROUPS):
+                for row in range(4):
+                    total = total + base[i, row, rows(g), :] * base[j, row, rows(g), :]
+            parts.append(jnp.sum(total, axis=0, keepdims=True))
+        whole = []
+        for (i, j), part in zip(PAIRS, parts):
+            for n in range(4):
+                square = scale[n] * seen[i][n] * seen[j][n]
+                part = part + square[:, :128] + square[:, 128:]
+            whole.append(part)
+        whole += parts[:3]
+        whole.append(jnp.zeros((16 - len(whole), 128), F32))
+        total = jnp.sum(jnp.concatenate(whole, axis=0), axis=1, keepdims=True)
+        mine = iota((16, 128), 0) == (iota((16, 128), 1) >> 3)
+        msg_a[...] = jnp.sum(jnp.where(mine, total, 0.0), axis=0, keepdims=True)
 
     def put_back(e):
         own = [[] for g in range(GROUPS)]
@@ -428,118 +418,72 @@
                     own[g].append(row[8 * g : 8 * g + 8])
         return own
 
-    def reduce_start(k, msg, slots, send_sem, recv_sem, offsets, mine, partner):
-        slots[k, mine] = msg[k]
-        for o in offsets:
+    def reduce_start(msg, slots, send_sem, recv_sem, size, mine, partner):
+        slots[mine] = msg[...]
+        for o in sorted(range(1, size), key=lambda o: -min(o, size - o)):
             pltpu.make_async_remote_copy(
-                src_ref=msg.at[k],
-                dst_ref=slots.at[k, mine],
-                send_sem=send_sem.at[k],
-                recv_sem=recv_sem.at[k],
+                src_ref=msg,
+                dst_ref=slots.at[mine],
+                send_sem=send_sem,
+                recv_sem=recv_sem,
                 device_id=partner(o),
                 device_id_type=MESH,
             ).start()
 
-    def all_of(k, slots, send_sem, recv_sem, count, partner):
-        several = slots.at[k, pl.ds(0, count - 1)]
+    def all_of(slots, send_sem, recv_sem, size, partner):
+        several = slots.at[pl.ds(0, size - 1)]
         return pltpu.make_async_remote_copy(
             src_ref=several,
             dst_ref=several,
-            send_sem=send_sem.at[k],
-            recv_sem=recv_sem.at[k],
+            send_sem=send_sem,
+            recv_sem=recv_sem,
             device_id=partner(1),
             device_id_type=MESH,
         )
 
-    def total_of(k, slots, count):
-        totals = [slots[k, o] for o in range(count)]
+    def total_of(slots, size):
+        totals = [slots[o] for o in range(size)]
         while len(totals) > 1:
             totals = [sum(totals[n : n + 2]) for n in range(0, len(totals), 2)]
         return totals[0]
 
-    def far_first(size):
-        return sorted(range(1, size), key=lambda o: -min(o, size - o))
-
     def over_y(o):
         return at(0, o)
 
     def over_x(o):
         return at(o, 0)
 
-    def start_a(k):
-        reduce_start(k, msg_a, slots_a, a_send, a_recv, far_first(ny), gy, over_y)
-
-    def turn(k):
-        all_of(k, slots_a, a_send, a_recv, ny, over_y).wait_recv()
-        msg_b[k] = total_of(k, slots_a, ny)
-        reduce_start(k, msg_b, slots_b, b_send, b_recv, far_first(nx), gx, over_x)
-
-    def end_b(k):
-        all_of(k, slots_b, b_send, b_recv, nx, over_x).wait_recv()
-        total = total_of(k, slots_b, nx)
-        total = jnp.sum(total, axis=1, keepdims=True)
-        gamma = jnp.broadcast_to(total[0:1], (8, 128))
-        return gamma, gamma + jnp.broadcast_to(total[1:2], (8, 128))
-
     copies = pack_and_send(0, own)
     arrived(copies)
-    smooth_step(0, None)
-    seen0 = observe()
-    values = squares(0, seen0, own_norm([]))
-    start_a(0)
-    scatter(values)
-    own = put_back(1)
-    copies = pack_and_send(1, own)
-    turn(0)
+    smooth_step(0)
+    seen = [observe()]
+    scatter(seen[0])
+    copies = pack_and_send(1, put_back(1))
     arrived(copies)
 
     rims = send(rim_rows(0))
-    smooth_step(1, None)
-    seen1 = observe()
-    gamma0, delta0 = end_b(0)
-    alpha0 = gamma0 / delta0
-    seen_r1 = [a - wide(alpha0) * b for a, b in zip(seen0, seen1)]
-    values = squares(1, seen_r1, own_norm([-alpha0]))
-    start_a(1)
-    scatter(values)
-    own = put_back(2)
-    copies = pack_and_send(2, own)
-    turn(1)
+    smooth_step(1)
+    seen.append(observe())
+    scatter(seen[1])
+    copies = pack_and_send(2, put_back(2))
     arrived(copies)
 
     rims += send(rim_rows(1))
-    smooth_step(2, alpha0)
+    smooth_step(2)
     edges = [
         [ured[1 + i, v, rows(g), :] for v in range(3) for i in range(4)] for g in range(GROUPS)
     ]
     pack(4, edges, 2, 32, 1)
-    rims += send(rim_rows(2) + side_moves(4))
-    seen2 = observe()
-    gamma1, delta1 = end_b(1)
-    beta1 = gamma1 / gamma0
-    alpha1 = gamma1 / (delta1 - beta1 * gamma1 / alpha0)
-    seen_r2 = [
-        a - wide(alpha1) * (b + wide(beta1) * c) for a, b, c in zip(seen_r1, seen2, seen1)
-    ]
-    of_r2 = [-alpha0 - alpha1 * beta1, -alpha1]
-    squares(2, seen_r2, own_norm(of_r2))
-    start_a(2)
-
-    both = 1.0 + beta1
-    factors = [
-        [alpha0 + alpha1 * both, -alpha1 * alpha0],
-        [jnp.ones((8, 128), F32)] + of_r2,
-        [both, -alpha0],
-    ]
-    for g in range(GROUPS):
+    rims += send(side_moves(4) + rim_rows(2))
+    seen.append(observe())
+    products(seen)
+    reduce_start(msg_a, slots_a, a_send, a_recv, ny, gy, over_y)
+
+    for v in range(3):
         for i in range(4):
-            for b in range(3):
-                ctl[b, i, rows(g), :] = sum(
-                    f * base_low[v, 2 + i, rows(g), :] for v, f in enumerate(factors[b])
-                )
+            ctl[v, i] = base[v, i]
     arrived(rims)
     tails = sides(4, 3, (lane8 & 1) == 1)
-    block = lane8 & 31
     out_row, in_col = iota((128, 48), 0), iota((128, 48), 1)
     off = (out_row & 15) - 4 * ((in_col >> 3) - 1)
     spread_x = jnp.where((in_col & 7) == (out_row >> 4), tap(off, 4), 0.0).astype(BF16)
@@ -547,68 +491,74 @@
     spread_y = tap(iota((256, 256), 1) - 2 * coarse_lane(iota((256, 256), 0)), 2).astype(BF16)
     sides_in = (lane8 == 0) | (lane8 == 127)
 
-    def interpolate(b):
-        most = factors[b] + [jnp.zeros((8, 128), F32)] * (3 - len(factors[b]))
-        of_lane = jnp.where(block < 8, most[0], jnp.where(block < 16, most[1], most[2]))
-        ends = []
-        for arrays in tails:
-            ends.append([])
-            for value in arrays:
-                value = value * of_lane
-                ends[-1].append(value + roll(value, -8) + roll(value, -16))
+    def interpolate(v):
         for g in range(GROUPS):
             for r in range(6):
-                value = sum(f * ured[r, v, rows(g), :] for v, f in enumerate(factors[b]))
+                value = ured[r, v, rows(g), :]
                 if r == 0:
                     value = jnp.where(left_f > 0.5, value, 0.0)
                 if r == 5:
                     value = jnp.where(right_f > 0.5, value, 0.0)
                 sx = 0 if r == 0 else 2 if r == 5 else 1
-                shift = 32 * (g % 4) + 2 * ((r - 1) % 4) + 1
-                end = jnp.where(sides_in, roll(ends[sx][g // 4], -shift), 0.0)
+                shift = 32 * (g % 4) + 8 * v + 2 * ((r - 1) % 4) + 1
+                end = jnp.where(sides_in, roll(tails[sx][g // 4], -shift), 0.0)
                 along[r, rows(g), :] = jnp.concatenate([value, end], axis=1)
         out = dot(pieces(along[...].reshape(6 * PAD, 256)), spread_y)
         out = (out[: 6 * PAD] + out[6 * PAD : 12 * PAD] + out[12 * PAD :]) * (1.0 / 60.0)
         out = out.reshape(6, PAD, 256)
         for g in range(GROUPS):
             part = dot(spread_x, pieces(out[:, 8 * g : 8 * g + 8, :].reshape(48, 256)))
-            fine[b, rows(g)] = part.reshape(8, 16, 256)
+            fine[v, rows(g)] = part.reshape(8, 16, 256)
 
     interpolate(0)
-    turn(2)
+    sums_a = all_of(slots_a, a_send, a_recv, ny, over_y)
+    sums_a.wait_recv()
+    msg_b[...] = total_of(slots_a, ny)
+    reduce_start(msg_b, slots_b, b_send, b_recv, nx, gx, over_x)
     interpolate(1)
     interpolate(2)
-    gamma2, delta2 = end_b(2)
-    beta2 = gamma2 / gamma1
-    alpha2 = gamma2 / (delta2 - beta2 * gamma2 / alpha1)
-    steps[0] = alpha2
-    steps[1] = alpha2 * beta2
+    sums_b = all_of(slots_b, b_send, b_recv, nx, over_x)
+    sums_b.wait_recv()
+    total = jnp.broadcast_to(total_of(slots_b, nx), (16, 128))
+    mine = iota((16, 128), 0) * 8 == iota((16, 128), 1)
+    total = jnp.sum(jnp.where(mine, total, 0.0), axis=1, keepdims=True)
+    m00, m01, m02, m11, m12, m22, b0, b1, b2 = [
+        jnp.broadcast_to(total[n : n + 1], (8, 128)) for n in range(9)
+    ]
+
+    def ratio(a, b):
+        return jnp.where(b > 0.0, a / jnp.where(b > 0.0, b, 1.0), 0.0)
+
+    l01, l02 = ratio(m01, m00), ratio(m02, m00)
+    m11, m12, m22 = m11 - l01 * m01, m12 - l01 * m02, m22 - l02 * m02
+    l12 = ratio(m12, m11)
+    b1, b2 = b1 - l01 * b0, b2 - l02 * b0
+    c2 = ratio(b2 - l12 * b1, m22 - l12 * m12)
+    c1 = ratio(b1, m11) - l12 * c2
+    steps[0] = ratio(b0, m00) - l01 * c1 - l02 * c2
+    steps[1] = c1
+    steps[2] = c2
 
     for dx, dy, copy in sent:
         pl.when(inside(dx, dy))(copy.wait_send)
-    for k in range(3):
-        all_of(k, slots_a, a_send, a_recv, ny, over_y).wait_send()
-        all_of(k, slots_b, b_send, b_recv, nx, over_x).wait_send()
+    sums_a.wait_send()
+    sums_b.wait_send()
 
 
 def finish(parts, ctl, steps, fine_hbm, control, fine, sems):
-    first, second = steps[0], steps[1]
-    first = jnp.concatenate([first, first], axis=1)
-    second = jnp.concatenate([second, second], axis=1)
+    each = [jnp.concatenate([steps[v], steps[v]], axis=1) for v in range(3)]
     copies = []
     for g in range(GROUPS):
         count = min(8, PLANES - 8 * g)
         for p in range(8 * g, 8 * g + count):
             for h in range(2):
                 at_h = pl.ds(8 * h, 8)
-                fine[p, at_h, :] = (
-                    parts[0, p, at_h, :] + first * parts[1, p, at_h, :] + second * parts[2, p, at_h, :]
-                )
+                fine[p, at_h, :] = sum(each[v] * parts[v, p, at_h, :] for v in range(3))
         planes = pl.ds(8 * g, count)
         copies.append(pltpu.make_async_copy(fine.at[planes], fine_hbm.at[planes], sems.at[g]))
         copies[-1].start()
     for i in range(4):
-        value = ctl[0, i] + steps[0][:1] * ctl[1, i] + steps[1][:1] * ctl[2, i]
+        value = sum(steps[v][:1] * ctl[v, i] for v in range(3))
         control[:, i, :] = value[:PLANES]
     for copy in copies:
         copy.wait()
@@ -624,7 +574,7 @@
         out_shape=[
             jax.ShapeDtypeStruct((3, PAD, 16, 256), F32),
             jax.ShapeDtypeStruct((3, 4, PAD, 128), F32),
-            jax.ShapeDtypeStruct((2, 8, 128), F32),
+            jax.ShapeDtypeStruct((3, 8, 128), F32),
         ],
         in_specs=[pl.BlockSpec(memory_space=pltpu.HBM)] * 8,
         out_specs=[vmem, vmem, vmem],
@@ -650,24 +600,23 @@
             pltpu.VMEM((3, 12, PAD, 128), F32),
             pltpu.VMEM((5, 24, 128), F32),
             pltpu.VMEM((5, 6, 24, 128), F32),
-            pltpu.VMEM((3, 8, PAD, 128), F32),
-            pltpu.VMEM((2, 8, PAD, 128), F32),
+            pltpu.VMEM((3, 4, PAD, 128), F32),
             pltpu.VMEM((6, 3, PAD, 128), F32),
             pltpu.VMEM((MPAD, 512), F32),
             pltpu.VMEM((3 * MPAD, 1024), BF16),
-            pltpu.VMEM((3, 2, 128), F32),
-            pltpu.VMEM((3, 2, 128), F32),
-            pltpu.VMEM((3, ny, 2, 128), F32),
-            pltpu.VMEM((3, nx, 2, 128), F32),
+            pltpu.VMEM((1, 128), F32),
+            pltpu.VMEM((1, 128), F32),
+            pltpu.VMEM((ny, 1, 128), F32),
+            pltpu.VMEM((nx, 1, 128), F32),
             dma((8,)),
             dma((7, 2)),
             dma((7, 2)),
             dma((5, 6)),
             dma((5, 6)),
-            dma((3,)),
-            dma((3,)),
-            dma((3,)),
-            dma((3,)),
+            dma,
+            dma,
+            dma,
+            dma,
         ],
         compiler_params=pltpu.CompilerParams(
             collective_id=0, has_side_effects=True, vmem_limit_bytes=40 << 20

time: 54.6 us -> 50.9 us (0.932)
  Pallas kernels: 53.9 us -> 50.2 us
    pallas_call x1, Pallas kernels: 52.2 us -> 48.4 us  [per_device(): pl.pallas_call(functools.partial(solve, nx, ny), out_shape=[jax.ShapeDtyp...]
where the time goes in v4:
time: 50.9 us; the launch traced here: 50.8 us
  Pallas kernels  50.2 us (99%)
  between operations  0.64 us (1%)
    pallas_call x1, Pallas kernels, per_device(): pl.pallas_call(functools.partial(solve, nx, ny), out_shape=[jax.ShapeDtyp...  48.4 us
    pallas_call x1, Pallas kernels, per_device(): pl.pallas_call(finish, out_shape=[jax.ShapeDtypeStruct((PLANES, 16, 256),...  1.74 us

profile of v4, /device:TPU:1, one launch (start us, length us, event | category | flops | bytes accessed | tf_op | source)
XLA Modules:
  0.0 50.8 jit_solution(18133296450850668864)
XLA Ops:
  0.6 48.4 %solve.1 = (f32[3,72,16,256]{3,2,1,0:T(8,128)S(1)}, f32[3,4,72,128]{3,2,1,0:T(8,128)S(1)}, f32[3,8,128]{2,1,0:T(8,128)S(1)}) custom-call(f32[68,16,256]{2,1,0:T(8,128)} %inn_hbm.1, f32[16,256]{1,0:T(8,128)} %area_hbm.1, f32[68,4,128]{2,1,0:T(4,128)} %sd_hbm.1, f32[1,68]{1,0:T(1,128)} %bitcast.7, s32[8,128]{1,0:T(8,128)} %bitcast.4, f32[68,1024]{1,0:T(8,128)} %weight_hbm.1, ...), custom_call_target="tpu_custom_call" | custom-call | tf_op jit(solution)/shard_map/solve/pallas_call | solution.py:572
  49.1 1.7 %finish.1 = (f32[68,16,256]{2,1,0:T(8,128)}, f32[68,4,128]{2,1,0:T(4,128)}) custom-call(f32[3,72,16,256]{3,2,1,0:T(8,128)S(1)} %get-tuple-element.5.parts, f32[3,4,72,128]{3,2,1,0:T(8,128)S(1)} %get-tuple-element.6.ctl, f32[3,8,128]{2,1,0:T(8,128)S(1)} %get-tuple-element.7.steps), custom_call_target="tpu_custom_call" | custom-call | tf_op jit(solution)/shard_map/finish/pallas_call | solution.py:640

commit v5 on v4

--- a/solution.py
+++ b/solution.py
@@ -94,6 +94,10 @@
     packed,
     packed_in,
     base,
+    base_high,
+    high_in,
+    once_low,
+    once_high,
     ured,
     gathered,
     scaled,
@@ -275,7 +279,9 @@
         return result
 
     copies = send(
-        side_moves(0) + row_moves(0, rest_low.at[0], rim_in.at[1], rest_low.at[5], rim_in.at[0])
+        side_moves(0)[:4]
+        + row_moves(0, rest_low.at[0], rim_in.at[1], rest_low.at[5], rim_in.at[0])
+        + side_moves(0)[4:]
     )
 
     for load in loads[2:]:
@@ -327,9 +333,14 @@
 
     def pack_and_send(e, parts):
         pack(1 + e, parts, 8, 32, 4)
-        own = field.at[e, pl.ds(4, 4)]
-        after, before = field.at[e, pl.ds(8, 4)], field.at[e, pl.ds(0, 4)]
-        return send(side_moves(1 + e) + row_moves(1 + e, own, after, own, before))
+        def part(r):
+            return field.at[e, pl.ds(r, 2)]
+
+        near = row_moves(1 + e, part(4), part(8), part(6), part(2))
+        far = row_moves(7 + e, part(6), part(10), part(4), part(0))
+        side = side_moves(1 + e)
+        copies = send(side[:4] + near + side[4:] + far)
+        return copies[:-2], copies[-2:]
 
     def smooth(rows, first, coefs):
         result = []
@@ -343,27 +354,48 @@
             result.append((a * low + b * of_low, a_high * high + b_high * of_high))
         return result
 
-    def smooth_step(e):
+    def coefficients(g):
+        a, b = coef_a[rows(g), :], coef_b[rows(g), :]
+        return [(a * f, b * f, a * f * edge_f, b * f * edge_f) for f in (left_f, F32(1.0), right_f)]
+
+    def line(e, g, r):
+        low = field[e, r, rows(g), :]
+        if r < 4:
+            low = jnp.where(left_f > 0.5, low, 0.0)
+        if r >= 8:
+            low = jnp.where(right_f > 0.5, low, 0.0)
+        return low
+
+    def side(tails, g, r):
+        return roll(tails[r // 4][g // 4], -(32 * (g % 4) + 8 * (r % 4) + 4))
+
+    def smooth_near(e):
         tails = sides(1 + e, 3, (lane8 & 4) == 4)
         for g in range(GROUPS):
-            at_g = rows(g)
-            lines = []
-            for r in range(12):
-                low = field[e, r, at_g, :]
-                if r < 4:
-                    low = jnp.where(left_f > 0.5, low, 0.0)
-                if r >= 8:
-                    low = jnp.where(right_f > 0.5, low, 0.0)
-                shift = 32 * (g % 4) + 8 * (r % 4) + 4
-                lines.append((low, roll(tails[r // 4][g // 4], -shift)))
-            a, b = coef_a[at_g, :], coef_b[at_g, :]
-            coefs = [
-                (a * f, b * f, a * f * edge_f, b * f * edge_f) for f in (left_f, F32(1.0), right_f)
-            ]
-            lines = smooth(smooth(lines, -4, coefs), -3, coefs)
-            for i in range(4):
-                base[e, i, at_g, :] = lines[2 + i][0]
-            values = smooth(smooth(lines, -2, coefs), -1, coefs)
+            at_g, coefs = rows(g), coefficients(g)
+            lines = [(line(e, g, r), side(tails, g, r)) for r in range(2, 10)]
+            for n, k in enumerate((0, 1, 6, 7)):
+                high_in[n, at_g, :] = lines[k][1]
+            once = smooth(lines, -2, coefs)
+            for n, k in enumerate((0, 1, 4, 5)):
+                once_low[n, at_g, :], once_high[n, at_g, :] = once[k]
+            for i, (low, high) in enumerate(smooth(once, -1, coefs)):
+                base[e, i, at_g, :] = low
+                base_high[i, at_g, :] = high
+
+    def smooth_far(e):
+        tails = sides(1 + e, 3, (lane8 & 4) == 4)
+        for g in range(GROUPS):
+            at_g, coefs = rows(g), coefficients(g)
+            above = [(line(e, g, r), side(tails, g, r)) for r in (0, 1)]
+            above += [(line(e, g, 2 + n), high_in[n, at_g, :]) for n in (0, 1)]
+            below = [(line(e, g, 6 + n), high_in[n, at_g, :]) for n in (2, 3)]
+            below += [(line(e, g, r), side(tails, g, r)) for r in (10, 11)]
+            once = [(once_low[n, at_g, :], once_high[n, at_g, :]) for n in range(4)]
+            above = smooth(smooth(above, -4, coefs) + once[:2], -3, coefs)
+            below = smooth(once[2:] + smooth(below, 4, coefs), 3, coefs)
+            own = [(base[e, i, at_g, :], base_high[i, at_g, :]) for i in range(4)]
+            values = smooth(smooth(above + own + below, -2, coefs), -1, coefs)
             for i, (low, _) in enumerate(values):
                 pushed = sd[i, at_g, :] * low
                 ured[1 + i, e, at_g, :] = pushed
@@ -453,23 +485,27 @@
     def over_x(o):
         return at(o, 0)
 
-    copies = pack_and_send(0, own)
-    arrived(copies)
-    smooth_step(0)
+    near, far = pack_and_send(0, own)
+    arrived(near)
+    smooth_near(0)
+    arrived(far)
+    smooth_far(0)
     seen = [observe()]
     scatter(seen[0])
-    copies = pack_and_send(1, put_back(1))
-    arrived(copies)
-
+    near, far = pack_and_send(1, put_back(1))
+    arrived(near)
+    smooth_near(1)
+    arrived(far)
     rims = send(rim_rows(0))
-    smooth_step(1)
+    smooth_far(1)
     seen.append(observe())
     scatter(seen[1])
-    copies = pack_and_send(2, put_back(2))
-    arrived(copies)
-
+    near, far = pack_and_send(2, put_back(2))
+    arrived(near)
+    smooth_near(2)
+    arrived(far)
     rims += send(rim_rows(1))
-    smooth_step(2)
+    smooth_far(2)
     edges = [
         [ured[1 + i, v, rows(g), :] for v in range(3) for i in range(4)] for g in range(GROUPS)
     ]
@@ -482,6 +518,10 @@
     for v in range(3):
         for i in range(4):
             ctl[v, i] = base[v, i]
+    sums_a = all_of(slots_a, a_send, a_recv, ny, over_y)
+    sums_a.wait_recv()
+    msg_b[...] = total_of(slots_a, ny)
+    reduce_start(msg_b, slots_b, b_send, b_recv, nx, gx, over_x)
     arrived(rims)
     tails = sides(4, 3, (lane8 & 1) == 1)
     out_row, in_col = iota((128, 48), 0), iota((128, 48), 1)
@@ -511,10 +551,6 @@
             fine[v, rows(g)] = part.reshape(8, 16, 256)
 
     interpolate(0)
-    sums_a = all_of(slots_a, a_send, a_recv, ny, over_y)
-    sums_a.wait_recv()
-    msg_b[...] = total_of(slots_a, ny)
-    reduce_start(msg_b, slots_b, b_send, b_recv, nx, gx, over_x)
     interpolate(1)
     interpolate(2)
     sums_b = all_of(slots_b, b_send, b_recv, nx, over_x)
@@ -601,6 +637,10 @@
             pltpu.VMEM((5, 24, 128), F32),
             pltpu.VMEM((5, 6, 24, 128), F32),
             pltpu.VMEM((3, 4, PAD, 128), F32),
+            pltpu.VMEM((4, PAD, 128), F32),
+            pltpu.VMEM((4, PAD, 128), F32),
+            pltpu.VMEM((4, PAD, 128), F32),
+            pltpu.VMEM((4, PAD, 128), F32),
             pltpu.VMEM((6, 3, PAD, 128), F32),
             pltpu.VMEM((MPAD, 512), F32),
             pltpu.VMEM((3 * MPAD, 1024), BF16),
@@ -609,8 +649,8 @@
             pltpu.VMEM((ny, 1, 128), F32),
             pltpu.VMEM((nx, 1, 128), F32),
             dma((8,)),
-            dma((7, 2)),
-            dma((7, 2)),
+            dma((10, 2)),
+            dma((10, 2)),
             dma((5, 6)),
             dma((5, 6)),
             dma,

time: 50.9 us -> 50.1 us (0.984)
  Pallas kernels: 50.2 us -> 49.4 us
    pallas_call x1, Pallas kernels: 48.4 us -> 47.7 us  [per_device(): pl.pallas_call(functools.partial(solve, nx, ny), out_shape=[jax.ShapeDtyp...]
where the time goes in v5:
time: 50.1 us; the launch traced here: 50 us
  Pallas kernels  49.4 us (99%)
  between operations  0.64 us (1%)
    pallas_call x1, Pallas kernels, per_device(): pl.pallas_call(functools.partial(solve, nx, ny), out_shape=[jax.ShapeDtyp...  47.7 us
    pallas_call x1, Pallas kernels, per_device(): pl.pallas_call(finish, out_shape=[jax.ShapeDtypeStruct((PLANES, 16, 256),...  1.74 us

profile of v5, /device:TPU:1, one launch (start us, length us, event | category | flops | bytes accessed | tf_op | source)
XLA Modules:
  0.0 50.0 jit_solution(4963519718385783776)
XLA Ops:
  0.6 47.7 %solve.1 = (f32[3,72,16,256]{3,2,1,0:T(8,128)S(1)}, f32[3,4,72,128]{3,2,1,0:T(8,128)S(1)}, f32[3,8,128]{2,1,0:T(8,128)S(1)}) custom-call(f32[68,16,256]{2,1,0:T(8,128)} %inn_hbm.1, f32[16,256]{1,0:T(8,128)} %area_hbm.1, f32[68,4,128]{2,1,0:T(4,128)} %sd_hbm.1, f32[1,68]{1,0:T(1,128)} %bitcast.7, s32[8,128]{1,0:T(8,128)} %bitcast.4, f32[68,1024]{1,0:T(8,128)} %weight_hbm.1, ...), custom_call_target="tpu_custom_call" | custom-call | tf_op jit(solution)/shard_map/solve/pallas_call | solution.py:608
  48.3 1.7 %finish.1 = (f32[68,16,256]{2,1,0:T(8,128)}, f32[68,4,128]{2,1,0:T(4,128)}) custom-call(f32[3,72,16,256]{3,2,1,0:T(8,128)S(1)} %get-tuple-element.5.parts, f32[3,4,72,128]{3,2,1,0:T(8,128)S(1)} %get-tuple-element.6.ctl, f32[3,8,128]{2,1,0:T(8,128)S(1)} %get-tuple-element.7.steps), custom_call_target="tpu_custom_call" | custom-call | tf_op jit(solution)/shard_map/finish/pallas_call | solution.py:680

commit v6 on v5

--- a/solution.py
+++ b/solution.py
@@ -190,7 +190,7 @@
     rest_low[...] = part[:, :128].reshape(6, PAD, 128)
     rest_high[...] = part[:, 128:].reshape(6, PAD, 128)
 
-    pack(0, [[rest_high[r, rows(g), :] for r in range(6)] for g in range(GROUPS)], 2, 16, 1)
+    pack(0, [[rest_high[r, rows(g), :] for r in range(6)] for g in range(GROUPS)], 2, 14, 1)
 
     pl.semaphore_wait(barrier, len(partners))
 
@@ -239,7 +239,7 @@
         ]
 
     def side_moves(e):
-        used = pl.ds(0, 16 if e == 0 else 24)
+        used = pl.ds(0, 8 if e == 0 else 24)
         return [
             (
                 -sx,
@@ -313,20 +313,20 @@
 
     arrived(copies)
 
-    rim = sides(0, 2, (lane8 & 1) == 0)
+    rim = sides(0, 1, (lane8 & 1) == 0)
     ends = (lane8 == 0) | (lane8 == 127)
     own = [[] for g in range(GROUPS)]
     for g in range(GROUPS):
-        v, first = g // 8, 16 * (g % 8) + 1
+        first = 14 * g + 1
         for i in range(4):
             value = rest_low[i + 1, rows(g), :]
-            tails = roll(rim[1][v], -(first + 2 * (i + 1)))
+            tails = roll(rim[1][0], -(first + 2 * (i + 1)))
             if i == 0:
                 value = value + jnp.where(left_f > 0.5, rim_in[0, rows(g), :], 0.0)
-                tails = tails + roll(rim[0][v], -(first + 10))
+                tails = tails + roll(rim[0][0], -(first + 10))
             if i == 3:
                 value = value + jnp.where(right_f > 0.5, rim_in[1, rows(g), :], 0.0)
-                tails = tails + roll(rim[2][v], -first)
+                tails = tails + roll(rim[2][0], -first)
             value = sd[i, rows(g), :] * (value + jnp.where(ends, tails, 0.0))
             field[0, 4 + i, rows(g), :] = value
             own[g].append(value)

time: 50.1 us -> 50.2 us (level)
  no operation moved by 1% of the time
where the time goes in v6:
time: 50.2 us; the launch traced here: 50.1 us
  Pallas kernels  49.4 us (98%)
  between operations  0.64 us (1%)
    pallas_call x1, Pallas kernels, per_device(): pl.pallas_call(functools.partial(solve, nx, ny), out_shape=[jax.ShapeDtyp...  47.7 us
    pallas_call x1, Pallas kernels, per_device(): pl.pallas_call(finish, out_shape=[jax.ShapeDtypeStruct((PLANES, 16, 256),...  1.74 us

profile of v6, /device:TPU:1, one launch (start us, length us, event | category | flops | bytes accessed | tf_op | source)
XLA Modules:
  0.0 50.1 jit_solution(8565061784285840466)
XLA Ops:
  0.6 47.7 %solve.1 = (f32[3,72,16,256]{3,2,1,0:T(8,128)S(1)}, f32[3,4,72,128]{3,2,1,0:T(8,128)S(1)}, f32[3,8,128]{2,1,0:T(8,128)S(1)}) custom-call(f32[68,16,256]{2,1,0:T(8,128)} %inn_hbm.1, f32[16,256]{1,0:T(8,128)} %area_hbm.1, f32[68,4,128]{2,1,0:T(4,128)} %sd_hbm.1, f32[1,68]{1,0:T(1,128)} %bitcast.7, s32[8,128]{1,0:T(8,128)} %bitcast.4, f32[68,1024]{1,0:T(8,128)} %weight_hbm.1, ...), custom_call_target="tpu_custom_call" | custom-call | tf_op jit(solution)/shard_map/solve/pallas_call | solution.py:608
  48.3 1.7 %finish.1 = (f32[68,16,256]{2,1,0:T(8,128)}, f32[68,4,128]{2,1,0:T(4,128)}) custom-call(f32[3,72,16,256]{3,2,1,0:T(8,128)S(1)} %get-tuple-element.5.parts, f32[3,4,72,128]{3,2,1,0:T(8,128)S(1)} %get-tuple-element.6.ctl, f32[3,8,128]{2,1,0:T(8,128)S(1)} %get-tuple-element.7.steps), custom_call_target="tpu_custom_call" | custom-call | tf_op jit(solution)/shard_map/finish/pallas_call | solution.py:680
